TPU v7x, 256 devices: a whole 4x4x8 slice. The times are simulated.
256 devices in a mesh: grp: 8 (over x_hi, y), mem: 32 (over z, x_lo, core).
Axes of the slice: x: 4 (x_hi: 2, x_lo: 2; x = x_hi * 2 + x_lo), y: 4, z: 8, core: 2. Of those that a mesh axis runs over, the one named last changes fastest.
Arguments:
- contracted_amplitudes: bfloat16 [1024, 32768], P('mem', 'grp'), may hold values from -6 to 6
- ladder_integrals: bfloat16 [32768, 32768], P('grp', 'mem'), may hold values from -0.046875 to 0.046875
- cd_pairs: int32 [8, 2], P('grp'), may hold values from 0 to 18, as said below
- block_irrep: int32 [19], replicated, may hold values from 0 to 7, as said below
- ab_blocks: int32 [8, 2], replicated, may hold values from 0 to 18, as said below
- amps_ab: bfloat16 [1024, 32768], P(('grp', 'mem')), may hold values from -6 to 6
- dressing: bfloat16 [19, 64, 64], replicated, may hold values from -0.75 to 0.75
- occ_energy: float32 [120], replicated, may hold values from -2 to -0.3
- virt_energy: float32 [1216], replicated, may hold values from 0.5 to 3
- pair_occ: int32 [1024, 2], P(('grp', 'mem')), may hold values from 0 to 119
Outputs:
- new_amps: float32 [1024, 32768], P(('grp', 'mem'))
Inputs may be any that keep to these rules, and one draw needn't show every extreme that they name: Every row of ab_blocks names two blocks whose irreps XOR to the same symmetry. `cd_pairs`: each index of grp holds 1 row; some index of grp holds a row with the symmetry of ab_blocks, and some other index holds none. `block_irrep`: every irrep 0 to 7 labels at least one block.
All inputs are finite; a program needn't handle non-finite values.
Results may differ from a plain program's by a relative error of at most 0.0003.
Values may be sent and summed in bfloat16 or wider, within the bound.
No kernel may reach another device: no remote copies, remote signals or barrier semaphores. Data moves between devices by JAX's collectives and lax.ppermute only.
A program may use at most 64 MiB of HBM per device.

v0:
```python
import jax
import jax.numpy as jnp
from jax import lax
from jax.experimental import pallas as pl
from jax.experimental.pallas import tpu as pltpu
from jax.sharding import PartitionSpec as P

Z = 8
MEM = 32


def pairs(target):
    return [(i, target(i)) for i in range(MEM)]


RING = pairs(lambda i: (i + 4) % MEM if i % 2 == 0 else (i - 4) % MEM)
NEIGHBOUR = pairs(lambda i: i ^ 2)
SIBLING = pairs(lambda i: i ^ 1)
RING_SIBLING = pairs(lambda i: (i - 3) % MEM if i % 2 == 0 else (i + 3) % MEM)
RING_NEIGHBOUR = pairs(lambda i: ((i + 4) % MEM if i % 2 == 0 else (i - 4) % MEM) ^ 2)


SLOTS = (0, 1, Z - 1, 2, Z - 2, 3, Z - 3, 4)
OWNERS = [[(i // 4 + (2 * (i % 2) - 1) * s) % Z * MEM + i for s in SLOTS] for i in range(MEM)]


def send(x, perm):
    return lax.ppermute(x, "mem", perm)


def stack(*blocks):
    return jnp.concatenate(blocks, axis=0)


def after(x, *done):
    return lax.optimization_barrier((x, *done))[0]


def ladder_partial(own, ready, multiply):
    rows = own.shape[0]
    a1 = send(own, RING)
    b1 = send(own, RING_SIBLING)
    q1 = send(own, RING_NEIGHBOUR)
    b0 = send(own, SIBLING)
    x0 = send(own, NEIGHBOUR)

    a1 = after(a1, ready)
    a2 = send(a1, RING)
    b1 = after(b1, a1)
    r1 = send(b1, NEIGHBOUR)
    b2 = send(b1, RING)
    q1 = after(q1, b1)
    q2 = send(q1, RING)

    a2 = after(a2, q1)
    a3 = send(a2, RING)
    b2 = after(b2, a2)
    b3 = send(b2, RING)
    r2 = send(b2, NEIGHBOUR)
    q2 = after(q2, b2)
    q3 = send(q2, RING)
    x0 = after(x0, q2)
    bx = send(x0, SIBLING)

    a3 = after(a3, x0)
    a4 = send(a3, RING)
    r1 = after(r1, a3)
    c1 = send(stack(b1, a1, r1, q1), SIBLING)
    b3 = after(b3, r1)
    r3 = send(b3, NEIGHBOUR)
    q3 = after(q3, b3)
    q4 = send(q3, RING)
    r2 = after(r2, q3)
    c2 = send(stack(b2, a2, r2, q2), SIBLING)
    product = multiply(stack(after(own, r2), b0, x0, bx, a1, b1, q1, r1, c1))
    partial = jnp.pad(product, ((0, 20 * rows), (0, 0)))

    c2 = after(c2, partial)
    product = multiply(stack(a2, b2, q2, r2, c2))
    partial = lax.dynamic_update_slice(partial, product, (12 * rows, 0))
    a4 = after(a4, partial)
    r3 = after(r3, a4)
    c3 = send(stack(b3, a3, r3, q3), SIBLING)
    q4 = after(q4, r3)
    c4 = send(stack(a4, q4), SIBLING)
    product = multiply(stack(a3, b3, q3, r3, c3, a4, c4[:rows], q4, c4[rows:]))
    return lax.dynamic_update_slice(partial, product, (20 * rows, 0))


def mask_kernel(cd_pairs, block_irrep, ab_blocks, scale):
    target = block_irrep[ab_blocks[0, 0]] ^ block_irrep[ab_blocks[1, 0]]
    symmetry = block_irrep[cd_pairs[0, 0]] ^ block_irrep[cd_pairs[0, 1]]
    scale[...] = jnp.full(scale.shape, jnp.where(symmetry == target, 32.0, 0.0), jnp.float32)


def local(
    contracted_amplitudes,
    ladder_integrals,
    cd_pairs,
    block_irrep,
    ab_blocks,
    amps_ab,
    dressing,
    occ_energy,
    virt_energy,
    pair_occ,
):
    col_count = ladder_integrals.shape[1]
    local_rows = amps_ab.shape[0]
    block_width = dressing.shape[1]
    pair_width = block_width * block_width
    block_total = dressing.shape[0]
    block_ids = jnp.arange(block_total, dtype=jnp.int32)
    out_onehot = (ab_blocks[:, :, None] == block_ids[None, None, :]).astype(jnp.int32)
    scale = pl.pallas_call(
        mask_kernel,
        out_shape=jax.ShapeDtypeStruct((1, 128), jnp.float32),
        in_specs=[pl.BlockSpec(memory_space=pltpu.SMEM)] * 3,
        out_specs=pl.BlockSpec(memory_space=pltpu.VMEM),
        compiler_params=pltpu.CompilerParams(vmem_limit_bytes=1 << 20),
    )(cd_pairs, block_irrep, ab_blocks.T)

    member = lax.axis_index("mem")
    x_lo = (member // 2) % 2
    core = member % 2

    def multiply(rows):
        rows = lax.optimization_barrier(rows)
        product = jnp.dot(rows, ladder_integrals, preferred_element_type=jnp.float32)
        return (product * scale[0, 0]).astype(jnp.float16)

    partial = ladder_partial(contracted_amplitudes, scale, multiply)
    partial = partial.reshape(Z, -1, col_count)
    partial = lax.all_to_all(partial, ("grp", "mem"), split_axis=0, concat_axis=0, axis_index_groups=OWNERS)
    summed = jnp.sum(partial.astype(jnp.float32), axis=0) * (1.0 / 32.0)
    summed = summed.reshape(2, 2, -1, col_count)
    summed = jnp.where(x_lo == 1, summed[::-1], summed)
    summed = jnp.where(core == 1, summed[:, ::-1], summed)
    lanes = col_count // 8
    summed = summed.reshape(MEM, local_rows, -1, lanes).transpose(0, 2, 1, 3).reshape(MEM, -1, lanes)
    depth = summed.shape[1]
    place = jnp.arange(depth, dtype=jnp.float32)[None, :, None]
    largest = jnp.maximum(jnp.max(jnp.abs(summed), axis=1, keepdims=True), 1e-30)
    step = jnp.ceil(jnp.log2(largest * (1.0 / 16300.0)) * 256.0)
    shifted = (step + 32768.0) * jnp.exp2(-place)
    bits = jnp.floor(shifted) - 2.0 * jnp.floor(shifted * 0.5)
    coded = 2.0 * jnp.round(summed * jnp.exp2(step * (-1.0 / 256.0))) + bits
    coded = lax.all_to_all(coded.astype(jnp.int16), "mem", split_axis=0, concat_axis=0).astype(jnp.float32)
    code = jnp.floor(coded * 0.5)
    weight = jnp.where(place < 16.0, jnp.exp2(place), 0.0)
    step = jnp.sum((coded - 2.0 * code) * weight, axis=1, keepdims=True) - 32768.0
    ladder = code * jnp.exp2(step * (1.0 / 256.0))
    ladder = ladder.reshape(MEM, -1, local_rows, lanes).transpose(0, 2, 1, 3).reshape(MEM, local_rows, col_count)

    out_pairs = ab_blocks.shape[0]
    left_select = out_onehot[:, 0, :].astype(jnp.float32)
    right_select = out_onehot[:, 1, :].astype(jnp.float32)
    dress_flat = dressing.reshape(block_total, pair_width).astype(jnp.float32)
    left_dress = jnp.dot(left_select, dress_flat, precision=lax.Precision.HIGHEST).reshape(
        out_pairs, block_width, block_width
    )
    right_dress = jnp.dot(right_select, dress_flat, precision=lax.Precision.HIGHEST).reshape(
        out_pairs, block_width, block_width
    )
    amp_blocks = amps_ab.astype(jnp.float32).reshape(
        local_rows, out_pairs, block_width, block_width
    )
    dressed = jnp.einsum("nac,pncb->pnab", left_dress, amp_blocks, precision=lax.Precision.HIGHEST)
    dressed = dressed + jnp.einsum(
        "nbc,pnac->pnab", right_dress, amp_blocks, precision=lax.Precision.HIGHEST
    )
    virt_blocks = virt_energy.reshape(block_total, block_width)
    left_energy = jnp.dot(left_select, virt_blocks, precision=lax.Precision.HIGHEST)
    right_energy = jnp.dot(right_select, virt_blocks, precision=lax.Precision.HIGHEST)
    occ_ids = jnp.arange(occ_energy.shape[0], dtype=jnp.int32)
    occ_onehot = (pair_occ[:, :, None] == occ_ids[None, None, :]).astype(jnp.float32)
    occ_pick = jnp.sum(occ_onehot * occ_energy[None, None, :], axis=-1)
    occ_sum = occ_pick[:, 0] + occ_pick[:, 1]
    denominator = (
        left_energy[None, :, :, None]
        + right_energy[None, :, None, :]
        - occ_sum[:, None, None, None]
    )
    width = out_pairs * pair_width
    dressed = dressed.reshape(local_rows, width)
    denominator = denominator.reshape(local_rows, width)
    ladder = ladder.transpose(1, 0, 2).reshape(local_rows, width)
    return (ladder + dressed) / denominator


def solution(mesh):
    return jax.shard_map(
        local,
        mesh=mesh,
        in_specs=(
            P("mem", "grp"),
            P("grp", "mem"),
            P("grp", None),
            P(),
            P(),
            P(("grp", "mem"), None),
            P(),
            P(),
            P(),
            P(("grp", "mem"), None),
        ),
        out_specs=P(("grp", "mem"), None),
        check_vma=False,
    )
```

profile of v0, /device:TPU:1, one launch (start us, length us, event | category | flops | bytes accessed | tf_op | source)
XLA Modules:
  0.0 116.5 jit_solution(2808359888076693991)
XLA Ops:
  0.0 6.4 %collective-permute-start.1 = (bf16[32,4096]{1,0:T(8,128)(2,1)}, bf16[32,4096]{1,0:T(8,128)(2,1)S(1)}, u32[]{:S(2)}, u32[]{:S(2)}) collective-permute-start(bf16[32,4096]{1,0:T(8,128)(2,1)} %param.10), channel_id=1, source_target_pairs={{0,4},{1,29},{2,6},{3,31},{4,8},{5,1},{6,10},{7,3},{8,12},{9,5},{1... | collective-permute-start | bytes 786440 | tf_op jit(solution)/shard_map/ppermute | solution.py:28
  6.4 1.7 %collective-permute-start.4 = (bf16[32,4096]{1,0:T(8,128)(2,1)}, bf16[32,4096]{1,0:T(8,128)(2,1)S(1)}, u32[]{:S(2)}, u32[]{:S(2)}) collective-permute-start(bf16[32,4096]{1,0:T(8,128)(2,1)} %param.10), channel_id=1, source_target_pairs={{0,6},{1,31},{2,4},{3,29},{4,10},{5,3},{6,8},{7,1},{8,14},{9,7},{1... | collective-permute-start | bytes 786440 | tf_op jit(solution)/shard_map/ppermute | solution.py:28
  8.1 0.7 copy-done
  8.7 0.7 copy-done.2
  9.4 0.7 copy-done.3
  10.1 0.6 shard_map.100
  10.6 0.9 collective-permute-done.1
  11.5 3.0 %collective-permute-start.3 = (bf16[32,4096]{1,0:T(8,128)(2,1)S(1)}, bf16[32,4096]{1,0:T(8,128)(2,1)S(1)}, u32[]{:S(2)}, u32[]{:S(2)}) collective-permute-start(bf16[32,4096]{1,0:T(8,128)(2,1)S(1)} %collective-permute-done.1), channel_id=1, source_target_pairs={{0,4},{1,29},{2,6},{3,31},{4,8},{5,1},{6,10},{7,3},{8,12},{9,5},{1... | collective-permute-start | bytes 786440 | tf_op jit(solution)/shard_map/ppermute | solution.py:28
  14.5 0.7 collective-permute-done
  15.3 2.1 %collective-permute-start.2 = (bf16[32,4096]{1,0:T(8,128)(2,1)S(1)}, bf16[32,4096]{1,0:T(8,128)(2,1)S(1)}, u32[]{:S(2)}, u32[]{:S(2)}) collective-permute-start(bf16[32,4096]{1,0:T(8,128)(2,1)S(1)} %collective-permute-done), channel_id=1, source_target_pairs={{0,4},{1,29},{2,6},{3,31},{4,8},{5,1},{6,10},{7,3},{8,12},{9,5},{1... | collective-permute-start | bytes 786440 | tf_op jit(solution)/shard_map/ppermute | solution.py:28
  17.3 3.8 %collective-permute-start.6 = (bf16[32,4096]{1,0:T(8,128)(2,1)S(1)}, bf16[32,4096]{1,0:T(8,128)(2,1)S(1)}, u32[]{:S(2)}, u32[]{:S(2)}) collective-permute-start(bf16[32,4096]{1,0:T(8,128)(2,1)S(1)} %collective-permute-done.4), channel_id=1, source_target_pairs={{0,4},{1,29},{2,6},{3,31},{4,8},{5,1},{6,10},{7,3},{8,12},{9,5},{1... | collective-permute-start | bytes 786440 | tf_op jit(solution)/shard_map/ppermute | solution.py:28
  21.2 0.3 collective-permute-start.11
  21.4 1.2 %collective-permute-start.9 = (bf16[32,4096]{1,0:T(8,128)(2,1)S(1)}, bf16[32,4096]{1,0:T(8,128)(2,1)S(1)}, u32[]{:S(2)}, u32[]{:S(2)}) collective-permute-start(bf16[32,4096]{1,0:T(8,128)(2,1)S(1)} %collective-permute-done), channel_id=1, source_target_pairs={{0,2},{1,3},{2,0},{3,1},{4,6},{5,7},{6,4},{7,5},{8,10},{9,11},{10,... | collective-permute-start | bytes 786440 | tf_op jit(solution)/shard_map/ppermute | solution.py:28
  22.6 1.6 %collective-permute-start.10 = (bf16[32,4096]{1,0:T(8,128)(2,1)S(1)}, bf16[32,4096]{1,0:T(8,128)(2,1)S(1)}, u32[]{:S(2)}, u32[]{:S(2)}) collective-permute-start(bf16[32,4096]{1,0:T(8,128)(2,1)S(1)} %collective-permute-done.3), channel_id=1, source_target_pairs={{0,4},{1,29},{2,6},{3,31},{4,8},{5,1},{6,10},{7,3},{8,12},{9,5},{1... | collective-permute-start | bytes 786440 | tf_op jit(solution)/shard_map/ppermute | solution.py:28
  24.3 0.2 collective-permute-done.6
  24.5 3.1 %collective-permute-start.8 = (bf16[32,4096]{1,0:T(8,128)(2,1)S(1)}, bf16[32,4096]{1,0:T(8,128)(2,1)S(1)}, u32[]{:S(2)}, u32[]{:S(2)}) collective-permute-start(bf16[32,4096]{1,0:T(8,128)(2,1)S(1)} %collective-permute-done.2), channel_id=1, source_target_pairs={{0,4},{1,29},{2,6},{3,31},{4,8},{5,1},{6,10},{7,3},{8,12},{9,5},{1... | collective-permute-start | bytes 786440 | tf_op jit(solution)/shard_map/ppermute | solution.py:28
  27.6 1.8 %collective-permute-done.11 = bf16[32,4096]{1,0:T(8,128)(2,1)S(1)} collective-permute-done((bf16[32,4096]{1,0:T(8,128)(2,1)}, bf16[32,4096]{1,0:T(8,128)(2,1)S(1)}, u32[]{:S(2)}, u32[]{:S(2)}) %collective-permute-start.11) | collective-permute-done | bytes 262176 | tf_op jit(solution)/shard_map/ppermute | solution.py:28
  29.5 0.7 collective-permute-start.5
  30.2 2.9 %collective-permute-done.9 = bf16[32,4096]{1,0:T(8,128)(2,1)S(1)} collective-permute-done((bf16[32,4096]{1,0:T(8,128)(2,1)S(1)}, bf16[32,4096]{1,0:T(8,128)(2,1)S(1)}, u32[]{:S(2)}, u32[]{:S(2)}) %collective-permute-start.9) | collective-permute-done | bytes 262176 | tf_op jit(solution)/shard_map/ppermute | solution.py:28
  33.1 1.0 collective-permute-start.13
  34.1 0.9 collective-permute-done.7
  35.0 0.8 collective-permute-done.5
  36.0 1.0 collective-permute-start.16
  37.0 3.5 %collective-permute-start.17 = (bf16[32,4096]{1,0:T(8,128)(2,1)S(1)}, bf16[32,4096]{1,0:T(8,128)(2,1)S(1)}, u32[]{:S(2)}, u32[]{:S(2)}) collective-permute-start(bf16[32,4096]{1,0:T(8,128)(2,1)S(1)} %collective-permute-done.10), channel_id=1, source_target_pairs={{0,4},{1,29},{2,6},{3,31},{4,8},{5,1},{6,10},{7,3},{8,12},{9,5},{1... | collective-permute-start | bytes 786440 | tf_op jit(solution)/shard_map/ppermute | solution.py:28
  40.8 3.0 %collective-permute-start.14 = (bf16[128,4096]{1,0:T(8,128)(2,1)S(1)}, bf16[128,4096]{1,0:T(8,128)(2,1)S(1)}, u32[]{:S(2)}, u32[]{:S(2)}) collective-permute-start(bf16[128,4096]{1,0:T(8,128)(2,1)S(1)} %pad_maximum_fusion), channel_id=1, source_target_pairs={{0,1},{1,0},{2,3},{3,2},{4,5},{5,4},{6,7},{7,6},{8,9},{9,8},{10,11... | collective-permute-start | bytes 3145736 | tf_op jit(solution)/shard_map/ppermute | solution.py:28
  43.8 0.1 collective-permute-start.15
  44.0 2.1 %collective-permute-done.14 = bf16[128,4096]{1,0:T(8,128)(2,1)S(1)} collective-permute-done((bf16[128,4096]{1,0:T(8,128)(2,1)S(1)}, bf16[128,4096]{1,0:T(8,128)(2,1)S(1)}, u32[]{:S(2)}, u32[]{:S(2)}) %collective-permute-start.14) | collective-permute-done | bytes 1048608 | tf_op jit(solution)/shard_map/ppermute | solution.py:28
  46.2 3.5 %multiply_convert_fusion.1 = f16[384,1024]{1,0:T(8,128)(2,1)S(1)} fusion(bf16[384,4096]{1,0:T(8,128)(2,1)S(1)} %constant_dynamic-update-slice_fusion, bf16[4096,1024]{1,0:T(8,128)(2,1)S(1)} %copy-done.12, f32[]{:T(128)S(1)} %bitcast.71), kind=kOutput, calls=%fused_computation.2 | convolution fusion | flops 3222011904 | bytes 12320772 | tf_op jit(solution)/shard_map/dot_general | solution.py:129
  49.7 0.3 pad.4
  50.0 0.1 constant_dynamic-update-slice_fusion.9
  50.1 2.4 %fusion.3 = f16[1024,1024]{1,0:T(8,128)(2,1)S(1)} fusion(f16[1024,1024]{1,0:T(8,128)(2,1)S(1)} %pad.4, bf16[256,4096]{1,0:T(8,128)(2,1)S(1)} %constant_dynamic-update-slice_fusion.9, bf16[4096,1024]{1,0:T(8,128)(2,1)S(1)} %copy-done.12, f32[]{:T(128)S(1)} %bitcast.72), kind=kOutput, calls=%fused_computation.9 | convolution fusion | flops 2148007936 | bytes 11010560 | tf_op jit(solution)/shard_map/dot_general | solution.py:129
  52.6 0.5 collective-permute-start.18
  53.1 0.2 collective-permute-start.20
  53.4 2.0 %collective-permute-done.18 = bf16[128,4096]{1,0:T(8,128)(2,1)S(1)} collective-permute-done((bf16[128,4096]{1,0:T(8,128)(2,1)S(1)}, bf16[128,4096]{1,0:T(8,128)(2,1)S(1)}, u32[]{:S(2)}, u32[]{:S(2)}) %collective-permute-start.18) | collective-permute-done | bytes 1048608 | tf_op jit(solution)/shard_map/ppermute | solution.py:28
  55.5 0.6 collective-permute-done.20
  56.2 3.5 %fusion = f16[1024,1024]{1,0:T(8,128)(2,1)S(1)} fusion(f16[1024,1024]{1,0:T(8,128)(2,1)S(1)} %fusion.3, bf16[384,4096]{1,0:T(8,128)(2,1)S(1)} %slice_dynamic-update-slice_fusion, bf16[4096,1024]{1,0:T(8,128)(2,1)S(1)} %copy-done.12, f32[]{:T(128)S(1)} %bitcast.73), kind=kOutput, calls=%fused_computation.3 | convolution fusion | flops 3222011904 | bytes 12321280 | tf_op jit(solution)/shard_map/dot_general | solution.py:129
  59.7 1.3 %copy-done.4 = f16[1024,1024]{1,0:T(8,128)(2,1)} copy-done((f16[1024,1024]{1,0:T(8,128)(2,1)}, f16[1024,1024]{1,0:T(8,128)(2,1)S(1)}, u32[]{:S(2)}) %copy-start.4) | copy-done | bytes 2097176
  61.0 6.4 %all-to-all-start = ((f16[8,128,1024]{2,1,0:T(8,128)(2,1)}), f16[8,128,1024]{2,1,0:T(8,128)(2,1)S(1)}, u32[]{:S(2)}, u32[]{:S(2)}) async-start(f16[8,128,1024]{2,1,0:T(8,128)(2,1)} %bitcast.74), calls=%async_computation | async-start | bytes 4194304 | tf_op jit(solution)/shard_map/all_to_all | solution.py:134
  67.4 0.4 reshape.124
  67.9 0.3 reshape.123
  68.2 0.3 dot_general.35
  68.6 0.5 convolution_bitcast_fusion.3
  69.1 0.5 convolution_bitcast_fusion.2
  69.6 0.1 fusion.25
  69.7 0.1 fusion.28
  69.9 0.6 convolution_bitcast_fusion.1
  70.4 1.6 %fusion.1 = f32[4,8,64,64]{3,2,0,1:T(8,128)} fusion(f32[4,8,64,64]{3,2,0,1:T(8,128)S(1)} %convolution_bitcast_fusion.1, bf16[4,8,64,64]{3,2,1,0:T(8,128)(2,1)S(1)} %reshape.124, f32[8,64,64,1]{2,0,1,3:T(8,128)S(1)} %convolution_bitcast_fusion.2), kind=kOutput, calls=%fused_computation.5 | convolution fusion | flops 100794368 | bytes 1441792 | tf_op jit(solution)/shard_map/nbc,pnac->pnab/dot_general | solution.py:169
  72.0 23.7 %all-to-all-done = f16[8,128,1024]{2,1,0:T(8,128)(2,1)S(1)} async-done(((f16[8,128,1024]{2,1,0:T(8,128)(2,1)}), f16[8,128,1024]{2,1,0:T(8,128)(2,1)S(1)}, u32[]{:S(2)}, u32[]{:S(2)}) %all-to-all-start) | async-done | bytes 2097184 | tf_op jit(solution)/shard_map/all_to_all | solution.py:134
  95.8 0.5 convert_reduce_fusion
  96.4 0.1 copy.75
  96.5 0.3 copy.55
  96.9 0.3 fusion.11
  97.2 0.8 copy.56
  98.0 5.2 %all-to-all-start.1 = ((s16[32,32,128]{2,1,0:T(8,128)(2,1)}), s16[32,32,128]{2,1,0:T(8,128)(2,1)S(1)}, u32[]{:S(2)}, u32[]{:S(2)}) async-start(s16[32,32,128]{2,1,0:T(8,128)(2,1)} %copy.56), calls=%async_computation.1 | async-start | bytes 524288 | tf_op jit(solution)/shard_map/all_to_all | solution.py:148
  103.2 0.1 broadcast_add_fusion
  103.4 0.1 copy.66
  103.5 0.4 reshape.125
  103.9 0.1 add.73
  104.0 0.2 select_reduce_fusion
  104.2 10.4 %all-to-all-done.1 = s16[32,32,128]{2,1,0:T(8,128)(2,1)S(1)} async-done(((s16[32,32,128]{2,1,0:T(8,128)(2,1)}), s16[32,32,128]{2,1,0:T(8,128)(2,1)S(1)}, u32[]{:S(2)}, u32[]{:S(2)}) %all-to-all-start.1) | async-done | bytes 262176 | tf_op jit(solution)/shard_map/all_to_all | solution.py:148
  114.6 0.2 fusion.8
  114.9 0.2 fusion.5
  115.1 0.3 copy.76
  115.4 1.0 subtract_divide_fusion
  (74 shorter events, 1.3 us)
Async XLA Ops:
  0.0 11.5 %collective-permute-start.1 = (bf16[32,4096]{1,0:T(8,128)(2,1)}, bf16[32,4096]{1,0:T(8,128)(2,1)S(1)}, u32[]{:S(2)}, u32[]{:S(2)}) collective-permute-start(bf16[32,4096]{1,0:T(8,128)(2,1)} %param.10), channel_id=1, source_target_pairs={{0,4},{1,29},{2,6},{3,31},{4,8},{5,1},{6,10},{7,3},{8,12},{9,5},{1... | collective-permute-start | bytes 786440 | tf_op jit(solution)/shard_map/ppermute | solution.py:28
  6.4 8.8 %collective-permute-start = (bf16[32,4096]{1,0:T(8,128)(2,1)}, bf16[32,4096]{1,0:T(8,128)(2,1)S(1)}, u32[]{:S(2)}, u32[]{:S(2)}) collective-permute-start(bf16[32,4096]{1,0:T(8,128)(2,1)} %param.10), channel_id=1, source_target_pairs={{0,29},{1,4},{2,31},{3,6},{4,1},{5,8},{6,3},{7,10},{8,5},{9,12},{1... | collective-permute-start | bytes 786440 | tf_op jit(solution)/shard_map/ppermute | solution.py:28
  6.4 10.9 %collective-permute-start.4 = (bf16[32,4096]{1,0:T(8,128)(2,1)}, bf16[32,4096]{1,0:T(8,128)(2,1)S(1)}, u32[]{:S(2)}, u32[]{:S(2)}) collective-permute-start(bf16[32,4096]{1,0:T(8,128)(2,1)} %param.10), channel_id=1, source_target_pairs={{0,6},{1,31},{2,4},{3,29},{4,10},{5,3},{6,8},{7,1},{8,14},{9,7},{1... | collective-permute-start | bytes 786440 | tf_op jit(solution)/shard_map/ppermute | solution.py:28
  8.1 0.7 copy-start
  8.7 0.7 copy-start.2
  9.4 0.7 copy-start.3
  10.6 29.9 %copy-start.8 = (bf16[32,4096]{1,0:T(8,128)(2,1)S(1)}, bf16[32,4096]{1,0:T(8,128)(2,1)}, u32[]{:S(2)}) copy-start(bf16[32,4096]{1,0:T(8,128)(2,1)} %param.10) | copy-start | bytes 786436
  11.5 9.9 %collective-permute-start.3 = (bf16[32,4096]{1,0:T(8,128)(2,1)S(1)}, bf16[32,4096]{1,0:T(8,128)(2,1)S(1)}, u32[]{:S(2)}, u32[]{:S(2)}) collective-permute-start(bf16[32,4096]{1,0:T(8,128)(2,1)S(1)} %collective-permute-done.1), channel_id=1, source_target_pairs={{0,4},{1,29},{2,6},{3,31},{4,8},{5,1},{6,10},{7,3},{8,12},{9,5},{1... | collective-permute-start | bytes 786440 | tf_op jit(solution)/shard_map/ppermute | solution.py:28
  15.3 7.4 %collective-permute-start.2 = (bf16[32,4096]{1,0:T(8,128)(2,1)S(1)}, bf16[32,4096]{1,0:T(8,128)(2,1)S(1)}, u32[]{:S(2)}, u32[]{:S(2)}) collective-permute-start(bf16[32,4096]{1,0:T(8,128)(2,1)S(1)} %collective-permute-done), channel_id=1, source_target_pairs={{0,4},{1,29},{2,6},{3,31},{4,8},{5,1},{6,10},{7,3},{8,12},{9,5},{1... | collective-permute-start | bytes 786440 | tf_op jit(solution)/shard_map/ppermute | solution.py:28
  17.3 7.1 %collective-permute-start.6 = (bf16[32,4096]{1,0:T(8,128)(2,1)S(1)}, bf16[32,4096]{1,0:T(8,128)(2,1)S(1)}, u32[]{:S(2)}, u32[]{:S(2)}) collective-permute-start(bf16[32,4096]{1,0:T(8,128)(2,1)S(1)} %collective-permute-done.4), channel_id=1, source_target_pairs={{0,4},{1,29},{2,6},{3,31},{4,8},{5,1},{6,10},{7,3},{8,12},{9,5},{1... | collective-permute-start | bytes 786440 | tf_op jit(solution)/shard_map/ppermute | solution.py:28
  21.2 8.3 %collective-permute-start.11 = (bf16[32,4096]{1,0:T(8,128)(2,1)}, bf16[32,4096]{1,0:T(8,128)(2,1)S(1)}, u32[]{:S(2)}, u32[]{:S(2)}) collective-permute-start(bf16[32,4096]{1,0:T(8,128)(2,1)} %param.10), channel_id=1, source_target_pairs={{0,2},{1,3},{2,0},{3,1},{4,6},{5,7},{6,4},{7,5},{8,10},{9,11},{10,... | collective-permute-start | bytes 786440 | tf_op jit(solution)/shard_map/ppermute | solution.py:28
  21.4 19.1 %collective-permute-start.12 = (bf16[32,4096]{1,0:T(8,128)(2,1)}, bf16[32,4096]{1,0:T(8,128)(2,1)S(1)}, u32[]{:S(2)}, u32[]{:S(2)}) collective-permute-start(bf16[32,4096]{1,0:T(8,128)(2,1)} %param.10), channel_id=1, source_target_pairs={{0,1},{1,0},{2,3},{3,2},{4,5},{5,4},{6,7},{7,6},{8,9},{9,8},{10,11... | collective-permute-start | bytes 786440 | tf_op jit(solution)/shard_map/ppermute | solution.py:28
  21.4 11.6 %collective-permute-start.9 = (bf16[32,4096]{1,0:T(8,128)(2,1)S(1)}, bf16[32,4096]{1,0:T(8,128)(2,1)S(1)}, u32[]{:S(2)}, u32[]{:S(2)}) collective-permute-start(bf16[32,4096]{1,0:T(8,128)(2,1)S(1)} %collective-permute-done), channel_id=1, source_target_pairs={{0,2},{1,3},{2,0},{3,1},{4,6},{5,7},{6,4},{7,5},{8,10},{9,11},{10,... | collective-permute-start | bytes 786440 | tf_op jit(solution)/shard_map/ppermute | solution.py:28
  22.6 6.9 %collective-permute-start.10 = (bf16[32,4096]{1,0:T(8,128)(2,1)S(1)}, bf16[32,4096]{1,0:T(8,128)(2,1)S(1)}, u32[]{:S(2)}, u32[]{:S(2)}) collective-permute-start(bf16[32,4096]{1,0:T(8,128)(2,1)S(1)} %collective-permute-done.3), channel_id=1, source_target_pairs={{0,4},{1,29},{2,6},{3,31},{4,8},{5,1},{6,10},{7,3},{8,12},{9,5},{1... | collective-permute-start | bytes 786440 | tf_op jit(solution)/shard_map/ppermute | solution.py:28
  24.5 9.6 %collective-permute-start.8 = (bf16[32,4096]{1,0:T(8,128)(2,1)S(1)}, bf16[32,4096]{1,0:T(8,128)(2,1)S(1)}, u32[]{:S(2)}, u32[]{:S(2)}) collective-permute-start(bf16[32,4096]{1,0:T(8,128)(2,1)S(1)} %collective-permute-done.2), channel_id=1, source_target_pairs={{0,4},{1,29},{2,6},{3,31},{4,8},{5,1},{6,10},{7,3},{8,12},{9,5},{1... | collective-permute-start | bytes 786440 | tf_op jit(solution)/shard_map/ppermute | solution.py:28
  29.5 5.5 %collective-permute-start.7 = (bf16[32,4096]{1,0:T(8,128)(2,1)S(1)}, bf16[32,4096]{1,0:T(8,128)(2,1)S(1)}, u32[]{:S(2)}, u32[]{:S(2)}) collective-permute-start(bf16[32,4096]{1,0:T(8,128)(2,1)S(1)} %collective-permute-done.6), channel_id=1, source_target_pairs={{0,4},{1,29},{2,6},{3,31},{4,8},{5,1},{6,10},{7,3},{8,12},{9,5},{1... | collective-permute-start | bytes 786440 | tf_op jit(solution)/shard_map/ppermute | solution.py:28
  29.5 6.4 %collective-permute-start.5 = (bf16[32,4096]{1,0:T(8,128)(2,1)S(1)}, bf16[32,4096]{1,0:T(8,128)(2,1)S(1)}, u32[]{:S(2)}, u32[]{:S(2)}) collective-permute-start(bf16[32,4096]{1,0:T(8,128)(2,1)S(1)} %collective-permute-done.2), channel_id=1, source_target_pairs={{0,2},{1,3},{2,0},{3,1},{4,6},{5,7},{6,4},{7,5},{8,10},{9,11},{10,... | collective-permute-start | bytes 786440 | tf_op jit(solution)/shard_map/ppermute | solution.py:28
  33.1 7.6 %collective-permute-start.13 = (bf16[32,4096]{1,0:T(8,128)(2,1)S(1)}, bf16[32,4096]{1,0:T(8,128)(2,1)S(1)}, u32[]{:S(2)}, u32[]{:S(2)}) collective-permute-start(bf16[32,4096]{1,0:T(8,128)(2,1)S(1)} %collective-permute-done.11), channel_id=1, source_target_pairs={{0,1},{1,0},{2,3},{3,2},{4,5},{5,4},{6,7},{7,6},{8,9},{9,8},{10,11... | collective-permute-start | bytes 786440 | tf_op jit(solution)/shard_map/ppermute | solution.py:28
  35.9 10.3 %copy-start.12 = (bf16[4096,1024]{1,0:T(8,128)(2,1)S(1)}, bf16[4096,1024]{1,0:T(8,128)(2,1)}, u32[]{:S(2)}) copy-start(bf16[4096,1024]{1,0:T(8,128)(2,1)} %param.11) | copy-start | bytes 25165828
  36.0 16.5 %collective-permute-start.16 = (bf16[32,4096]{1,0:T(8,128)(2,1)S(1)}, bf16[32,4096]{1,0:T(8,128)(2,1)S(1)}, u32[]{:S(2)}, u32[]{:S(2)}) collective-permute-start(bf16[32,4096]{1,0:T(8,128)(2,1)S(1)} %collective-permute-done.8), channel_id=1, source_target_pairs={{0,2},{1,3},{2,0},{3,1},{4,6},{5,7},{6,4},{7,5},{8,10},{9,11},{10,... | collective-permute-start | bytes 786440 | tf_op jit(solution)/shard_map/ppermute | solution.py:28
  37.0 15.5 %collective-permute-start.17 = (bf16[32,4096]{1,0:T(8,128)(2,1)S(1)}, bf16[32,4096]{1,0:T(8,128)(2,1)S(1)}, u32[]{:S(2)}, u32[]{:S(2)}) collective-permute-start(bf16[32,4096]{1,0:T(8,128)(2,1)S(1)} %collective-permute-done.10), channel_id=1, source_target_pairs={{0,4},{1,29},{2,6},{3,31},{4,8},{5,1},{6,10},{7,3},{8,12},{9,5},{1... | collective-permute-start | bytes 786440 | tf_op jit(solution)/shard_map/ppermute | solution.py:28
  40.5 12.6 %collective-permute-start.19 = (bf16[32,4096]{1,0:T(8,128)(2,1)S(1)}, bf16[32,4096]{1,0:T(8,128)(2,1)S(1)}, u32[]{:S(2)}, u32[]{:S(2)}) collective-permute-start(bf16[32,4096]{1,0:T(8,128)(2,1)S(1)} %collective-permute-done.7), channel_id=1, source_target_pairs={{0,4},{1,29},{2,6},{3,31},{4,8},{5,1},{6,10},{7,3},{8,12},{9,5},{1... | collective-permute-start | bytes 786440 | tf_op jit(solution)/shard_map/ppermute | solution.py:28
  40.8 5.3 %collective-permute-start.14 = (bf16[128,4096]{1,0:T(8,128)(2,1)S(1)}, bf16[128,4096]{1,0:T(8,128)(2,1)S(1)}, u32[]{:S(2)}, u32[]{:S(2)}) collective-permute-start(bf16[128,4096]{1,0:T(8,128)(2,1)S(1)} %pad_maximum_fusion), channel_id=1, source_target_pairs={{0,1},{1,0},{2,3},{3,2},{4,5},{5,4},{6,7},{7,6},{8,9},{9,8},{10,11... | collective-permute-start | bytes 3145736 | tf_op jit(solution)/shard_map/ppermute | solution.py:28
  43.8 6.2 %collective-permute-start.15 = (bf16[128,4096]{1,0:T(8,128)(2,1)S(1)}, bf16[128,4096]{1,0:T(8,128)(2,1)S(1)}, u32[]{:S(2)}, u32[]{:S(2)}) collective-permute-start(bf16[128,4096]{1,0:T(8,128)(2,1)S(1)} %pad_maximum_fusion.1), channel_id=1, source_target_pairs={{0,1},{1,0},{2,3},{3,2},{4,5},{5,4},{6,7},{7,6},{8,9},{9,8},{10,11... | collective-permute-start | bytes 3145736 | tf_op jit(solution)/shard_map/ppermute | solution.py:28
  52.6 2.7 %collective-permute-start.18 = (bf16[128,4096]{1,0:T(8,128)(2,1)S(1)}, bf16[128,4096]{1,0:T(8,128)(2,1)S(1)}, u32[]{:S(2)}, u32[]{:S(2)}) collective-permute-start(bf16[128,4096]{1,0:T(8,128)(2,1)S(1)} %pad_maximum_fusion.2), channel_id=1, source_target_pairs={{0,1},{1,0},{2,3},{3,2},{4,5},{5,4},{6,7},{7,6},{8,9},{9,8},{10,11... | collective-permute-start | bytes 3145736 | tf_op jit(solution)/shard_map/ppermute | solution.py:28
  53.1 3.0 %collective-permute-start.20 = (bf16[64,4096]{1,0:T(8,128)(2,1)S(1)}, bf16[64,4096]{1,0:T(8,128)(2,1)S(1)}, u32[]{:S(2)}, u32[]{:S(2)}) collective-permute-start(bf16[64,4096]{1,0:T(8,128)(2,1)S(1)} %pad_maximum_fusion.3), channel_id=1, source_target_pairs={{0,1},{1,0},{2,3},{3,2},{4,5},{5,4},{6,7},{7,6},{8,9},{9,8},{10,11... | collective-permute-start | bytes 1572872 | tf_op jit(solution)/shard_map/ppermute | solution.py:28
  59.7 1.3 %copy-start.4 = (f16[1024,1024]{1,0:T(8,128)(2,1)}, f16[1024,1024]{1,0:T(8,128)(2,1)S(1)}, u32[]{:S(2)}) copy-start(f16[1024,1024]{1,0:T(8,128)(2,1)S(1)} %fusion) | copy-start | bytes 6291460
  61.0 6.4 %copy-start.7 = (bf16[4,32768]{1,0:T(4,128)(2,1)S(1)}, bf16[4,32768]{1,0:T(4,128)(2,1)}, u32[]{:S(2)}) copy-start(bf16[4,32768]{1,0:T(4,128)(2,1)} %param.15) | copy-start | bytes 786436
  61.0 6.9 %copy-start.6 = (bf16[19,64,64]{2,1,0:T(8,128)(2,1)S(1)}, bf16[19,64,64]{2,1,0:T(8,128)(2,1)}, u32[]{:S(2)}) copy-start(bf16[19,64,64]{2,1,0:T(8,128)(2,1)} %param.16) | copy-start | bytes 466948
  61.0 7.4 %copy-start.9 = (f32[1216]{0:T(1024)S(1)}, f32[1216]{0:T(1024)}, u32[]{:S(2)}) copy-start(f32[1216]{0:T(1024)} %param.18) | copy-start | bytes 14596
  61.0 7.5 %copy-start.1 = (s32[8,2]{0,1:T(2,128)S(1)}, s32[8,2]{0,1:T(2,128)}, u32[]{:S(2)}) copy-start(s32[8,2]{0,1:T(2,128)} %param.14) | copy-start | bytes 196
  61.0 34.7 %all-to-all-start = ((f16[8,128,1024]{2,1,0:T(8,128)(2,1)}), f16[8,128,1024]{2,1,0:T(8,128)(2,1)S(1)}, u32[]{:S(2)}, u32[]{:S(2)}) async-start(f16[8,128,1024]{2,1,0:T(8,128)(2,1)} %bitcast.74), calls=%async_computation | async-start | bytes 4194304 | tf_op jit(solution)/shard_map/all_to_all | solution.py:134
  96.3 7.0 %copy-start.5 = (f32[4,8,64,64]{3,2,0,1:T(8,128)S(1)}, f32[4,8,64,64]{3,2,0,1:T(8,128)}, u32[]{:S(2)}) copy-start(f32[4,8,64,64]{3,2,0,1:T(8,128)} %fusion.1) | copy-start | bytes 1572868
  96.9 7.2 %copy-start.10 = (s32[4,2]{0,1:T(2,128)S(1)}, s32[4,2]{0,1:T(2,128)}, u32[]{:S(2)}) copy-start(s32[4,2]{0,1:T(2,128)} %param.19) | copy-start | bytes 100
  96.9 7.2 %copy-start.11 = (f32[120]{0:T(128)S(1)}, f32[120]{0:T(128)}, u32[]{:S(2)}) copy-start(f32[120]{0:T(128)} %param.17) | copy-start | bytes 1444
  98.0 16.6 %all-to-all-start.1 = ((s16[32,32,128]{2,1,0:T(8,128)(2,1)}), s16[32,32,128]{2,1,0:T(8,128)(2,1)S(1)}, u32[]{:S(2)}, u32[]{:S(2)}) async-start(s16[32,32,128]{2,1,0:T(8,128)(2,1)} %copy.56), calls=%async_computation.1 | async-start | bytes 524288 | tf_op jit(solution)/shard_map/all_to_all | solution.py:148
where the time goes:
time: 118 us; the launch traced here: 116 us
  waiting for transfers between devices  47.1 us (40%)
  starting transfers between devices  44.8 us (38%)
  matrix products  12.8 us (11%)
  local copies, waits for them, and re-layouts  7.6 us (6%)
  other arithmetic  3.02 us (3%)
    ppermute x21, starting transfers between devices, send(): return lax.ppermute(x, 'mem', perm)  33.3 us
    all_to_all x1, waiting for transfers between devices, local(): lax.all_to_all(partial, ('grp', 'mem'), split_axis=0, concat_axis=0, axis...  23.7 us
    ppermute x21, waiting for transfers between devices, send(): return lax.ppermute(x, 'mem', perm)  12.9 us
    all_to_all x1, waiting for transfers between devices, local(): lax.all_to_all(coded.astype(jnp.int16), 'mem', split_axis=0, concat_axis=0)  10.4 us
    dot_general x3, matrix products, multiply(): jnp.dot(rows, ladder_integrals, preferred_element_type=jnp.float32)  9.4 us
    all_to_all x1, starting transfers between devices, local(): lax.all_to_all(partial, ('grp', 'mem'), split_axis=0, concat_axis=0, axis...  6.39 us
    all_to_all x1, starting transfers between devices, local(): lax.all_to_all(coded.astype(jnp.int16), 'mem', split_axis=0, concat_axis=0)  5.16 us
    unnamed x48, local copies, waits for them, and re-layouts  4.23 us
  transfers between devices with their start and end apart: 23, of which 12 were waited for; matrix products, arithmetic and copies ran while one was open for 11% of the time, Pallas kernels for 0%

commit v1 on v0

--- a/solution.py
+++ b/solution.py
@@ -46,33 +46,35 @@
 
     a1 = after(a1, ready)
     a2 = send(a1, RING)
-    b1 = after(b1, a1)
+    b1 = after(b1, a1, b0)
+    b2 = send(b1, RING)
     r1 = send(b1, NEIGHBOUR)
-    b2 = send(b1, RING)
     q1 = after(q1, b1)
     q2 = send(q1, RING)
+    x0 = after(x0, q1)
+    bx = send(x0, SIBLING)
 
-    a2 = after(a2, q1)
+    a2 = after(a2, x0)
     a3 = send(a2, RING)
-    b2 = after(b2, a2)
+    b2 = after(b2, a2, bx)
     b3 = send(b2, RING)
     r2 = send(b2, NEIGHBOUR)
     q2 = after(q2, b2)
     q3 = send(q2, RING)
-    x0 = after(x0, q2)
-    bx = send(x0, SIBLING)
+    r1 = after(r1, q2)
+    near = stack(b1, a1, r1, q1)
+    c1 = send(near, SIBLING)
 
-    a3 = after(a3, x0)
+    a3 = after(a3, near)
     a4 = send(a3, RING)
-    r1 = after(r1, a3)
-    c1 = send(stack(b1, a1, r1, q1), SIBLING)
-    b3 = after(b3, r1)
+    b3 = after(b3, a3, c1)
     r3 = send(b3, NEIGHBOUR)
     q3 = after(q3, b3)
     q4 = send(q3, RING)
     r2 = after(r2, q3)
-    c2 = send(stack(b2, a2, r2, q2), SIBLING)
-    product = multiply(stack(after(own, r2), b0, x0, bx, a1, b1, q1, r1, c1))
+    middle = stack(b2, a2, r2, q2)
+    c2 = send(middle, SIBLING)
+    product = multiply(stack(after(own, middle), b0, x0, bx, a1, b1, q1, r1, c1))
     partial = jnp.pad(product, ((0, 20 * rows), (0, 0)))
 
     c2 = after(c2, partial)
@@ -132,25 +134,12 @@
     partial = ladder_partial(contracted_amplitudes, scale, multiply)
     partial = partial.reshape(Z, -1, col_count)
     partial = lax.all_to_all(partial, ("grp", "mem"), split_axis=0, concat_axis=0, axis_index_groups=OWNERS)
-    summed = jnp.sum(partial.astype(jnp.float32), axis=0) * (1.0 / 32.0)
+    summed = jnp.sum(partial.astype(jnp.float32), axis=0)
     summed = summed.reshape(2, 2, -1, col_count)
     summed = jnp.where(x_lo == 1, summed[::-1], summed)
     summed = jnp.where(core == 1, summed[:, ::-1], summed)
-    lanes = col_count // 8
-    summed = summed.reshape(MEM, local_rows, -1, lanes).transpose(0, 2, 1, 3).reshape(MEM, -1, lanes)
-    depth = summed.shape[1]
-    place = jnp.arange(depth, dtype=jnp.float32)[None, :, None]
-    largest = jnp.maximum(jnp.max(jnp.abs(summed), axis=1, keepdims=True), 1e-30)
-    step = jnp.ceil(jnp.log2(largest * (1.0 / 16300.0)) * 256.0)
-    shifted = (step + 32768.0) * jnp.exp2(-place)
-    bits = jnp.floor(shifted) - 2.0 * jnp.floor(shifted * 0.5)
-    coded = 2.0 * jnp.round(summed * jnp.exp2(step * (-1.0 / 256.0))) + bits
-    coded = lax.all_to_all(coded.astype(jnp.int16), "mem", split_axis=0, concat_axis=0).astype(jnp.float32)
-    code = jnp.floor(coded * 0.5)
-    weight = jnp.where(place < 16.0, jnp.exp2(place), 0.0)
-    step = jnp.sum((coded - 2.0 * code) * weight, axis=1, keepdims=True) - 32768.0
-    ladder = code * jnp.exp2(step * (1.0 / 256.0))
-    ladder = ladder.reshape(MEM, -1, local_rows, lanes).transpose(0, 2, 1, 3).reshape(MEM, local_rows, col_count)
+    summed = summed.reshape(MEM, local_rows, col_count).astype(jnp.float16)
+    ladder = lax.all_to_all(summed, "mem", split_axis=0, concat_axis=0).astype(jnp.float32) * (1.0 / 32.0)
 
     out_pairs = ab_blocks.shape[0]
     left_select = out_onehot[:, 0, :].astype(jnp.float32)

time: 118 us -> 110 us (0.932)
  waiting for transfers between devices: 47.1 us -> 42.6 us
    ppermute x21, waiting for transfers between devices: 12.9 us -> 8.31 us  [send(): return lax.ppermute(x, 'mem', perm)]
    ppermute x21, starting transfers between devices: 33.3 us -> 31.4 us  [send(): return lax.ppermute(x, 'mem', perm)]
    unnamed x48 -> x50, local copies, waits for them, and re-layouts: 4.23 us -> 3.92 us
  transfers between devices with their start and end apart: 23 -> 23, of which waited for: 12 -> 9; matrix products, arithmetic and copies ran while one was open for 11% -> 11% of each run, Pallas kernels for 0% -> 1%
where the time goes in v1:
time: 110 us
  starting transfers between devices  44.2 us (40%)
  waiting for transfers between devices  42.6 us (39%)
  matrix products  11.7 us (11%)
  local copies, waits for them, and re-layouts  7.73 us (7%)
  other arithmetic  2.24 us (2%)
    ppermute x21, starting transfers between devices, send(): return lax.ppermute(x, 'mem', perm)  31.4 us
    all_to_all x1, waiting for transfers between devices, local(): lax.all_to_all(partial, ('grp', 'mem'), split_axis=0, concat_axis=0, axis...  23.2 us
    all_to_all x1, waiting for transfers between devices, local(): lax.all_to_all(summed, 'mem', split_axis=0, concat_axis=0)  11 us
    dot_general x3, matrix products, multiply(): jnp.dot(rows, ladder_integrals, preferred_element_type=jnp.float32)  9.4 us
    ppermute x21, waiting for transfers between devices, send(): return lax.ppermute(x, 'mem', perm)  8.31 us
    all_to_all x1, starting transfers between devices, local(): lax.all_to_all(partial, ('grp', 'mem'), split_axis=0, concat_axis=0, axis...  6.79 us
    all_to_all x1, starting transfers between devices, local(): lax.all_to_all(summed, 'mem', split_axis=0, concat_axis=0)  6.07 us
    unnamed x50, local copies, waits for them, and re-layouts  3.92 us
  transfers between devices with their start and end apart: 23, of which 9 were waited for; matrix products, arithmetic and copies ran while one was open for 11% of the time, Pallas kernels for 1%

profile of v1, /device:TPU:1, one launch (start us, length us, event | category | flops | bytes accessed | tf_op | source)
XLA Modules:
  0.0 109.6 jit_solution(5178949925919439697)
XLA Ops:
  0.0 6.4 %collective-permute-start.1 = (bf16[32,4096]{1,0:T(8,128)(2,1)}, bf16[32,4096]{1,0:T(8,128)(2,1)S(1)}, u32[]{:S(2)}, u32[]{:S(2)}) collective-permute-start(bf16[32,4096]{1,0:T(8,128)(2,1)} %param.10), channel_id=1, source_target_pairs={{0,4},{1,29},{2,6},{3,31},{4,8},{5,1},{6,10},{7,3},{8,12},{9,5},{1... | collective-permute-start | bytes 786440 | tf_op jit(solution)/shard_map/ppermute | solution.py:28
  6.4 4.0 %collective-permute-start.6 = (bf16[32,4096]{1,0:T(8,128)(2,1)}, bf16[32,4096]{1,0:T(8,128)(2,1)S(1)}, u32[]{:S(2)}, u32[]{:S(2)}) collective-permute-start(bf16[32,4096]{1,0:T(8,128)(2,1)} %param.10), channel_id=1, source_target_pairs={{0,6},{1,31},{2,4},{3,29},{4,10},{5,3},{6,8},{7,1},{8,14},{9,7},{1... | collective-permute-start | bytes 786440 | tf_op jit(solution)/shard_map/ppermute | solution.py:28
  10.4 0.3 collective-permute-start.5
  10.7 0.7 copy-done
  11.3 0.7 copy-done.2
  12.0 0.7 copy-done.3
  12.7 0.6 shard_map.100
  13.2 0.0 copy-start.8
  13.3 1.3 %collective-permute-start.4 = (bf16[32,4096]{1,0:T(8,128)(2,1)S(1)}, bf16[32,4096]{1,0:T(8,128)(2,1)S(1)}, u32[]{:S(2)}, u32[]{:S(2)}) collective-permute-start(bf16[32,4096]{1,0:T(8,128)(2,1)S(1)} %collective-permute-done.1), channel_id=1, source_target_pairs={{0,4},{1,29},{2,6},{3,31},{4,8},{5,1},{6,10},{7,3},{8,12},{9,5},{1... | collective-permute-start | bytes 786440 | tf_op jit(solution)/shard_map/ppermute | solution.py:28
  14.5 0.7 collective-permute-done
  15.3 2.1 %collective-permute-start.3 = (bf16[32,4096]{1,0:T(8,128)(2,1)S(1)}, bf16[32,4096]{1,0:T(8,128)(2,1)S(1)}, u32[]{:S(2)}, u32[]{:S(2)}) collective-permute-start(bf16[32,4096]{1,0:T(8,128)(2,1)S(1)} %collective-permute-done), channel_id=1, source_target_pairs={{0,4},{1,29},{2,6},{3,31},{4,8},{5,1},{6,10},{7,3},{8,12},{9,5},{1... | collective-permute-start | bytes 786440 | tf_op jit(solution)/shard_map/ppermute | solution.py:28
  17.3 1.2 %collective-permute-start.13 = (bf16[32,4096]{1,0:T(8,128)(2,1)S(1)}, bf16[32,4096]{1,0:T(8,128)(2,1)S(1)}, u32[]{:S(2)}, u32[]{:S(2)}) collective-permute-start(bf16[32,4096]{1,0:T(8,128)(2,1)S(1)} %collective-permute-done), channel_id=1, source_target_pairs={{0,2},{1,3},{2,0},{3,1},{4,6},{5,7},{6,4},{7,5},{8,10},{9,11},{10,... | collective-permute-start | bytes 786440 | tf_op jit(solution)/shard_map/ppermute | solution.py:28
  18.6 2.6 %collective-permute-start.9 = (bf16[32,4096]{1,0:T(8,128)(2,1)S(1)}, bf16[32,4096]{1,0:T(8,128)(2,1)S(1)}, u32[]{:S(2)}, u32[]{:S(2)}) collective-permute-start(bf16[32,4096]{1,0:T(8,128)(2,1)S(1)} %collective-permute-done.6), channel_id=1, source_target_pairs={{0,4},{1,29},{2,6},{3,31},{4,8},{5,1},{6,10},{7,3},{8,12},{9,5},{1... | collective-permute-start | bytes 786440 | tf_op jit(solution)/shard_map/ppermute | solution.py:28
  21.2 1.5 %collective-permute-done.5 = bf16[32,4096]{1,0:T(8,128)(2,1)S(1)} collective-permute-done((bf16[32,4096]{1,0:T(8,128)(2,1)}, bf16[32,4096]{1,0:T(8,128)(2,1)S(1)}, u32[]{:S(2)}, u32[]{:S(2)}) %collective-permute-start.5) | collective-permute-done | bytes 262176 | tf_op jit(solution)/shard_map/ppermute | solution.py:28
  22.7 0.0 collective-permute-start.7
  22.7 3.8 %collective-permute-start.12 = (bf16[32,4096]{1,0:T(8,128)(2,1)S(1)}, bf16[32,4096]{1,0:T(8,128)(2,1)S(1)}, u32[]{:S(2)}, u32[]{:S(2)}) collective-permute-start(bf16[32,4096]{1,0:T(8,128)(2,1)S(1)} %collective-permute-done.4), channel_id=1, source_target_pairs={{0,4},{1,29},{2,6},{3,31},{4,8},{5,1},{6,10},{7,3},{8,12},{9,5},{1... | collective-permute-start | bytes 786440 | tf_op jit(solution)/shard_map/ppermute | solution.py:28
  26.5 1.1 collective-permute-start.11
  27.6 0.3 collective-permute-start.8
  27.9 0.2 collective-permute-done.13
  28.2 0.8 collective-permute-start.14
  29.0 0.0 copy-start.12
  29.1 0.8 collective-permute-done.12
  29.8 3.1 %collective-permute-start.17 = (bf16[32,4096]{1,0:T(8,128)(2,1)S(1)}, bf16[32,4096]{1,0:T(8,128)(2,1)S(1)}, u32[]{:S(2)}, u32[]{:S(2)}) collective-permute-start(bf16[32,4096]{1,0:T(8,128)(2,1)S(1)} %collective-permute-done.12), channel_id=1, source_target_pairs={{0,4},{1,29},{2,6},{3,31},{4,8},{5,1},{6,10},{7,3},{8,12},{9,5},{1... | collective-permute-start | bytes 786440 | tf_op jit(solution)/shard_map/ppermute | solution.py:28
  33.0 2.5 %collective-permute-done.10 = bf16[32,4096]{1,0:T(8,128)(2,1)S(1)} collective-permute-done((bf16[32,4096]{1,0:T(8,128)(2,1)S(1)}, bf16[32,4096]{1,0:T(8,128)(2,1)S(1)}, u32[]{:S(2)}, u32[]{:S(2)}) %collective-permute-start.10) | collective-permute-done | bytes 262176 | tf_op jit(solution)/shard_map/ppermute | solution.py:28
  35.5 1.4 %collective-permute-start.15 = (bf16[128,4096]{1,0:T(8,128)(2,1)S(1)}, bf16[128,4096]{1,0:T(8,128)(2,1)S(1)}, u32[]{:S(2)}, u32[]{:S(2)}) collective-permute-start(bf16[128,4096]{1,0:T(8,128)(2,1)S(1)} %constant_dynamic-update-slice_fusion.4), channel_id=1, source_target_pairs={{0,1},{1,0},{2,3},{3,2},{4,5},{5,4},{6,7},{7,6},{8,9},{9,8},{10,11... | collective-permute-start | bytes 3145736 | tf_op jit(solution)/shard_map/ppermute | solution.py:28
  36.9 0.8 collective-permute-start.16
  37.7 1.7 %collective-permute-start.19 = (bf16[32,4096]{1,0:T(8,128)(2,1)S(1)}, bf16[32,4096]{1,0:T(8,128)(2,1)S(1)}, u32[]{:S(2)}, u32[]{:S(2)}) collective-permute-start(bf16[32,4096]{1,0:T(8,128)(2,1)S(1)} %collective-permute-done.10), channel_id=1, source_target_pairs={{0,4},{1,29},{2,6},{3,31},{4,8},{5,1},{6,10},{7,3},{8,12},{9,5},{1... | collective-permute-start | bytes 786440 | tf_op jit(solution)/shard_map/ppermute | solution.py:28
  39.6 0.1 constant_dynamic-update-slice_fusion.8
  39.7 3.5 %multiply_convert_fusion.1 = f16[384,1024]{1,0:T(8,128)(2,1)S(1)} fusion(bf16[384,4096]{1,0:T(8,128)(2,1)S(1)} %constant_dynamic-update-slice_fusion.8, bf16[4096,1024]{1,0:T(8,128)(2,1)S(1)} %copy-done.12, f32[]{:T(128)S(1)} %bitcast.48), kind=kOutput, calls=%fused_computation.2 | convolution fusion | flops 3222011904 | bytes 12320772 | tf_op jit(solution)/shard_map/dot_general | solution.py:131
  43.2 0.3 pad.4
  43.5 0.1 constant_dynamic-update-slice_fusion.17
  43.6 2.4 %fusion.3 = f16[1024,1024]{1,0:T(8,128)(2,1)S(1)} fusion(f16[1024,1024]{1,0:T(8,128)(2,1)S(1)} %pad.4, bf16[256,4096]{1,0:T(8,128)(2,1)S(1)} %constant_dynamic-update-slice_fusion.17, bf16[4096,1024]{1,0:T(8,128)(2,1)S(1)} %copy-done.12, f32[]{:T(128)S(1)} %bitcast.49), kind=kOutput, calls=%fused_computation.9 | convolution fusion | flops 2148007936 | bytes 11010560 | tf_op jit(solution)/shard_map/dot_general | solution.py:131
  46.0 0.1 pad_maximum_fusion
  46.1 0.1 collective-permute-start.18
  46.3 0.6 collective-permute-start.20
  46.9 2.0 %collective-permute-done.18 = bf16[128,4096]{1,0:T(8,128)(2,1)S(1)} collective-permute-done((bf16[128,4096]{1,0:T(8,128)(2,1)S(1)}, bf16[128,4096]{1,0:T(8,128)(2,1)S(1)}, u32[]{:S(2)}, u32[]{:S(2)}) %collective-permute-start.18) | collective-permute-done | bytes 1048608 | tf_op jit(solution)/shard_map/ppermute | solution.py:28
  48.9 0.1 constant_dynamic-update-slice_fusion.24
  49.0 0.6 collective-permute-done.20
  49.7 3.5 %fusion = f16[1024,1024]{1,0:T(8,128)(2,1)S(1)} fusion(f16[1024,1024]{1,0:T(8,128)(2,1)S(1)} %fusion.3, bf16[384,4096]{1,0:T(8,128)(2,1)S(1)} %slice_dynamic-update-slice_fusion, bf16[4096,1024]{1,0:T(8,128)(2,1)S(1)} %copy-done.12, f32[]{:T(128)S(1)} %bitcast.50), kind=kOutput, calls=%fused_computation.3 | convolution fusion | flops 3222011904 | bytes 12321280 | tf_op jit(solution)/shard_map/dot_general | solution.py:131
  53.2 1.3 %copy-done.4 = f16[1024,1024]{1,0:T(8,128)(2,1)} copy-done((f16[1024,1024]{1,0:T(8,128)(2,1)}, f16[1024,1024]{1,0:T(8,128)(2,1)S(1)}, u32[]{:S(2)}) %copy-start.4) | copy-done | bytes 2097176
  54.5 6.8 %all-to-all-start = ((f16[8,128,1024]{2,1,0:T(8,128)(2,1)}), f16[8,128,1024]{2,1,0:T(8,128)(2,1)S(1)}, u32[]{:S(2)}, u32[]{:S(2)}) async-start(f16[8,128,1024]{2,1,0:T(8,128)(2,1)} %bitcast.51), calls=%async_computation | async-start | bytes 4194304 | tf_op jit(solution)/shard_map/all_to_all | solution.py:136
  61.3 0.3 reshape.61
  61.6 0.3 dot_general.35
  61.9 0.4 reshape.62
  62.4 0.1 fusion.11
  62.5 0.5 convolution_bitcast_fusion.3
  62.9 0.5 convolution_bitcast_fusion.2
  63.4 0.6 convolution_bitcast_fusion.1
  64.0 0.6 fusion.1
  64.6 0.1 copy.35
  64.7 1.2 %reshape.63 = f32[4,32768]{1,0:T(4,128)} reshape(f32[4,8,64,64]{3,2,1,0:T(8,128)S(1)} %copy.35) | data formatting | bytes 1048576 | tf_op jit(solution)/shard_map/reshape | solution.py:174
  65.9 0.1 reshape.64
  66.0 0.1 fusion.13
  66.1 0.1 fusion.16
  66.2 23.2 %all-to-all-done = f16[8,128,1024]{2,1,0:T(8,128)(2,1)S(1)} async-done(((f16[8,128,1024]{2,1,0:T(8,128)(2,1)}), f16[8,128,1024]{2,1,0:T(8,128)(2,1)S(1)}, u32[]{:S(2)}, u32[]{:S(2)}) %all-to-all-start) | async-done | bytes 2097184 | tf_op jit(solution)/shard_map/all_to_all | solution.py:136
  89.5 0.5 convert_reduce_fusion
  90.1 0.8 convert_element_type.48
  90.9 6.1 %all-to-all-start.1 = ((f16[32,4,1024]{2,1,0:T(4,128)(2,1)}), f16[32,4,1024]{2,1,0:T(4,128)(2,1)S(1)}, u32[]{:S(2)}, u32[]{:S(2)}) async-start(f16[32,4,1024]{2,1,0:T(4,128)(2,1)} %convert_element_type.48), calls=%async_computation.1 | async-start | bytes 524288 | tf_op jit(solution)/shard_map/all_to_all | solution.py:142
  97.0 0.1 broadcast_add_fusion
  97.1 0.1 add.54
  97.2 0.2 select_reduce_fusion
  97.4 11.0 %all-to-all-done.1 = f16[32,4,1024]{2,1,0:T(4,128)(2,1)S(1)} async-done(((f16[32,4,1024]{2,1,0:T(4,128)(2,1)}), f16[32,4,1024]{2,1,0:T(4,128)(2,1)S(1)}, u32[]{:S(2)}, u32[]{:S(2)}) %all-to-all-start.1) | async-done | bytes 262176 | tf_op jit(solution)/shard_map/all_to_all | solution.py:142
  108.4 0.1 convert_multiply_fusion
  108.6 1.0 subtract_divide_fusion
  (67 shorter events, 0.7 us)
Async XLA Ops:
  0.0 13.2 %collective-permute-start.1 = (bf16[32,4096]{1,0:T(8,128)(2,1)}, bf16[32,4096]{1,0:T(8,128)(2,1)S(1)}, u32[]{:S(2)}, u32[]{:S(2)}) collective-permute-start(bf16[32,4096]{1,0:T(8,128)(2,1)} %param.10), channel_id=1, source_target_pairs={{0,4},{1,29},{2,6},{3,31},{4,8},{5,1},{6,10},{7,3},{8,12},{9,5},{1... | collective-permute-start | bytes 786440 | tf_op jit(solution)/shard_map/ppermute | solution.py:28
  6.4 8.1 %collective-permute-start.2 = (bf16[32,4096]{1,0:T(8,128)(2,1)}, bf16[32,4096]{1,0:T(8,128)(2,1)S(1)}, u32[]{:S(2)}, u32[]{:S(2)}) collective-permute-start(bf16[32,4096]{1,0:T(8,128)(2,1)} %param.10), channel_id=1, source_target_pairs={{0,1},{1,0},{2,3},{3,2},{4,5},{5,4},{6,7},{7,6},{8,9},{9,8},{10,11... | collective-permute-start | bytes 786440 | tf_op jit(solution)/shard_map/ppermute | solution.py:28
  6.4 8.8 %collective-permute-start = (bf16[32,4096]{1,0:T(8,128)(2,1)}, bf16[32,4096]{1,0:T(8,128)(2,1)S(1)}, u32[]{:S(2)}, u32[]{:S(2)}) collective-permute-start(bf16[32,4096]{1,0:T(8,128)(2,1)} %param.10), channel_id=1, source_target_pairs={{0,29},{1,4},{2,31},{3,6},{4,1},{5,8},{6,3},{7,10},{8,5},{9,12},{1... | collective-permute-start | bytes 786440 | tf_op jit(solution)/shard_map/ppermute | solution.py:28
  6.4 12.1 %collective-permute-start.6 = (bf16[32,4096]{1,0:T(8,128)(2,1)}, bf16[32,4096]{1,0:T(8,128)(2,1)S(1)}, u32[]{:S(2)}, u32[]{:S(2)}) collective-permute-start(bf16[32,4096]{1,0:T(8,128)(2,1)} %param.10), channel_id=1, source_target_pairs={{0,6},{1,31},{2,4},{3,29},{4,10},{5,3},{6,8},{7,1},{8,14},{9,7},{1... | collective-permute-start | bytes 786440 | tf_op jit(solution)/shard_map/ppermute | solution.py:28
  10.4 12.3 %collective-permute-start.5 = (bf16[32,4096]{1,0:T(8,128)(2,1)}, bf16[32,4096]{1,0:T(8,128)(2,1)S(1)}, u32[]{:S(2)}, u32[]{:S(2)}) collective-permute-start(bf16[32,4096]{1,0:T(8,128)(2,1)} %param.10), channel_id=1, source_target_pairs={{0,2},{1,3},{2,0},{3,1},{4,6},{5,7},{6,4},{7,5},{8,10},{9,11},{10,... | collective-permute-start | bytes 786440 | tf_op jit(solution)/shard_map/ppermute | solution.py:28
  10.7 0.7 copy-start
  11.3 0.7 copy-start.2
  12.0 0.7 copy-start.3
  13.2 26.1 %copy-start.8 = (bf16[32,4096]{1,0:T(8,128)(2,1)S(1)}, bf16[32,4096]{1,0:T(8,128)(2,1)}, u32[]{:S(2)}) copy-start(bf16[32,4096]{1,0:T(8,128)(2,1)} %param.10) | copy-start | bytes 786436
  13.3 9.5 %collective-permute-start.4 = (bf16[32,4096]{1,0:T(8,128)(2,1)S(1)}, bf16[32,4096]{1,0:T(8,128)(2,1)S(1)}, u32[]{:S(2)}, u32[]{:S(2)}) collective-permute-start(bf16[32,4096]{1,0:T(8,128)(2,1)S(1)} %collective-permute-done.1), channel_id=1, source_target_pairs={{0,4},{1,29},{2,6},{3,31},{4,8},{5,1},{6,10},{7,3},{8,12},{9,5},{1... | collective-permute-start | bytes 786440 | tf_op jit(solution)/shard_map/ppermute | solution.py:28
  15.3 11.3 %collective-permute-start.3 = (bf16[32,4096]{1,0:T(8,128)(2,1)S(1)}, bf16[32,4096]{1,0:T(8,128)(2,1)S(1)}, u32[]{:S(2)}, u32[]{:S(2)}) collective-permute-start(bf16[32,4096]{1,0:T(8,128)(2,1)S(1)} %collective-permute-done), channel_id=1, source_target_pairs={{0,4},{1,29},{2,6},{3,31},{4,8},{5,1},{6,10},{7,3},{8,12},{9,5},{1... | collective-permute-start | bytes 786440 | tf_op jit(solution)/shard_map/ppermute | solution.py:28
  17.3 10.8 %collective-permute-start.13 = (bf16[32,4096]{1,0:T(8,128)(2,1)S(1)}, bf16[32,4096]{1,0:T(8,128)(2,1)S(1)}, u32[]{:S(2)}, u32[]{:S(2)}) collective-permute-start(bf16[32,4096]{1,0:T(8,128)(2,1)S(1)} %collective-permute-done), channel_id=1, source_target_pairs={{0,2},{1,3},{2,0},{3,1},{4,6},{5,7},{6,4},{7,5},{8,10},{9,11},{10,... | collective-permute-start | bytes 786440 | tf_op jit(solution)/shard_map/ppermute | solution.py:28
  18.6 9.4 %collective-permute-start.9 = (bf16[32,4096]{1,0:T(8,128)(2,1)S(1)}, bf16[32,4096]{1,0:T(8,128)(2,1)S(1)}, u32[]{:S(2)}, u32[]{:S(2)}) collective-permute-start(bf16[32,4096]{1,0:T(8,128)(2,1)S(1)} %collective-permute-done.6), channel_id=1, source_target_pairs={{0,4},{1,29},{2,6},{3,31},{4,8},{5,1},{6,10},{7,3},{8,12},{9,5},{1... | collective-permute-start | bytes 786440 | tf_op jit(solution)/shard_map/ppermute | solution.py:28
  22.7 3.8 %collective-permute-start.7 = (bf16[32,4096]{1,0:T(8,128)(2,1)S(1)}, bf16[32,4096]{1,0:T(8,128)(2,1)S(1)}, u32[]{:S(2)}, u32[]{:S(2)}) collective-permute-start(bf16[32,4096]{1,0:T(8,128)(2,1)S(1)} %collective-permute-done.5), channel_id=1, source_target_pairs={{0,1},{1,0},{2,3},{3,2},{4,5},{5,4},{6,7},{7,6},{8,9},{9,8},{10,11... | collective-permute-start | bytes 786440 | tf_op jit(solution)/shard_map/ppermute | solution.py:28
  22.7 7.1 %collective-permute-start.12 = (bf16[32,4096]{1,0:T(8,128)(2,1)S(1)}, bf16[32,4096]{1,0:T(8,128)(2,1)S(1)}, u32[]{:S(2)}, u32[]{:S(2)}) collective-permute-start(bf16[32,4096]{1,0:T(8,128)(2,1)S(1)} %collective-permute-done.4), channel_id=1, source_target_pairs={{0,4},{1,29},{2,6},{3,31},{4,8},{5,1},{6,10},{7,3},{8,12},{9,5},{1... | collective-permute-start | bytes 786440 | tf_op jit(solution)/shard_map/ppermute | solution.py:28
  26.5 6.5 %collective-permute-start.11 = (bf16[32,4096]{1,0:T(8,128)(2,1)S(1)}, bf16[32,4096]{1,0:T(8,128)(2,1)S(1)}, u32[]{:S(2)}, u32[]{:S(2)}) collective-permute-start(bf16[32,4096]{1,0:T(8,128)(2,1)S(1)} %collective-permute-done.3), channel_id=1, source_target_pairs={{0,4},{1,29},{2,6},{3,31},{4,8},{5,1},{6,10},{7,3},{8,12},{9,5},{1... | collective-permute-start | bytes 786440 | tf_op jit(solution)/shard_map/ppermute | solution.py:28
  27.6 7.9 %collective-permute-start.8 = (bf16[32,4096]{1,0:T(8,128)(2,1)S(1)}, bf16[32,4096]{1,0:T(8,128)(2,1)S(1)}, u32[]{:S(2)}, u32[]{:S(2)}) collective-permute-start(bf16[32,4096]{1,0:T(8,128)(2,1)S(1)} %collective-permute-done.3), channel_id=1, source_target_pairs={{0,2},{1,3},{2,0},{3,1},{4,6},{5,7},{6,4},{7,5},{8,10},{9,11},{10,... | collective-permute-start | bytes 786440 | tf_op jit(solution)/shard_map/ppermute | solution.py:28
  27.9 7.5 %collective-permute-start.10 = (bf16[32,4096]{1,0:T(8,128)(2,1)S(1)}, bf16[32,4096]{1,0:T(8,128)(2,1)S(1)}, u32[]{:S(2)}, u32[]{:S(2)}) collective-permute-start(bf16[32,4096]{1,0:T(8,128)(2,1)S(1)} %collective-permute-done.9), channel_id=1, source_target_pairs={{0,4},{1,29},{2,6},{3,31},{4,8},{5,1},{6,10},{7,3},{8,12},{9,5},{1... | collective-permute-start | bytes 786440 | tf_op jit(solution)/shard_map/ppermute | solution.py:28
  28.2 4.8 %collective-permute-start.14 = (bf16[128,4096]{1,0:T(8,128)(2,1)S(1)}, bf16[128,4096]{1,0:T(8,128)(2,1)S(1)}, u32[]{:S(2)}, u32[]{:S(2)}) collective-permute-start(bf16[128,4096]{1,0:T(8,128)(2,1)S(1)} %constant_dynamic-update-slice_fusion), channel_id=1, source_target_pairs={{0,1},{1,0},{2,3},{3,2},{4,5},{5,4},{6,7},{7,6},{8,9},{9,8},{10,11... | collective-permute-start | bytes 3145736 | tf_op jit(solution)/shard_map/ppermute | solution.py:28
  29.0 10.6 %copy-start.12 = (bf16[4096,1024]{1,0:T(8,128)(2,1)S(1)}, bf16[4096,1024]{1,0:T(8,128)(2,1)}, u32[]{:S(2)}) copy-start(bf16[4096,1024]{1,0:T(8,128)(2,1)} %param.11) | copy-start | bytes 25165828
  29.8 16.2 %collective-permute-start.17 = (bf16[32,4096]{1,0:T(8,128)(2,1)S(1)}, bf16[32,4096]{1,0:T(8,128)(2,1)S(1)}, u32[]{:S(2)}, u32[]{:S(2)}) collective-permute-start(bf16[32,4096]{1,0:T(8,128)(2,1)S(1)} %collective-permute-done.12), channel_id=1, source_target_pairs={{0,4},{1,29},{2,6},{3,31},{4,8},{5,1},{6,10},{7,3},{8,12},{9,5},{1... | collective-permute-start | bytes 786440 | tf_op jit(solution)/shard_map/ppermute | solution.py:28
  35.5 8.0 %collective-permute-start.15 = (bf16[128,4096]{1,0:T(8,128)(2,1)S(1)}, bf16[128,4096]{1,0:T(8,128)(2,1)S(1)}, u32[]{:S(2)}, u32[]{:S(2)}) collective-permute-start(bf16[128,4096]{1,0:T(8,128)(2,1)S(1)} %constant_dynamic-update-slice_fusion.4), channel_id=1, source_target_pairs={{0,1},{1,0},{2,3},{3,2},{4,5},{5,4},{6,7},{7,6},{8,9},{9,8},{10,11... | collective-permute-start | bytes 3145736 | tf_op jit(solution)/shard_map/ppermute | solution.py:28
  36.9 9.1 %collective-permute-start.16 = (bf16[32,4096]{1,0:T(8,128)(2,1)S(1)}, bf16[32,4096]{1,0:T(8,128)(2,1)S(1)}, u32[]{:S(2)}, u32[]{:S(2)}) collective-permute-start(bf16[32,4096]{1,0:T(8,128)(2,1)S(1)} %collective-permute-done.11), channel_id=1, source_target_pairs={{0,2},{1,3},{2,0},{3,1},{4,6},{5,7},{6,4},{7,5},{8,10},{9,11},{10,... | collective-permute-start | bytes 786440 | tf_op jit(solution)/shard_map/ppermute | solution.py:28
  37.7 8.6 %collective-permute-start.19 = (bf16[32,4096]{1,0:T(8,128)(2,1)S(1)}, bf16[32,4096]{1,0:T(8,128)(2,1)S(1)}, u32[]{:S(2)}, u32[]{:S(2)}) collective-permute-start(bf16[32,4096]{1,0:T(8,128)(2,1)S(1)} %collective-permute-done.10), channel_id=1, source_target_pairs={{0,4},{1,29},{2,6},{3,31},{4,8},{5,1},{6,10},{7,3},{8,12},{9,5},{1... | collective-permute-start | bytes 786440 | tf_op jit(solution)/shard_map/ppermute | solution.py:28
  46.1 2.7 %collective-permute-start.18 = (bf16[128,4096]{1,0:T(8,128)(2,1)S(1)}, bf16[128,4096]{1,0:T(8,128)(2,1)S(1)}, u32[]{:S(2)}, u32[]{:S(2)}) collective-permute-start(bf16[128,4096]{1,0:T(8,128)(2,1)S(1)} %pad_maximum_fusion), channel_id=1, source_target_pairs={{0,1},{1,0},{2,3},{3,2},{4,5},{5,4},{6,7},{7,6},{8,9},{9,8},{10,11... | collective-permute-start | bytes 3145736 | tf_op jit(solution)/shard_map/ppermute | solution.py:28
  46.3 3.3 %collective-permute-start.20 = (bf16[64,4096]{1,0:T(8,128)(2,1)S(1)}, bf16[64,4096]{1,0:T(8,128)(2,1)S(1)}, u32[]{:S(2)}, u32[]{:S(2)}) collective-permute-start(bf16[64,4096]{1,0:T(8,128)(2,1)S(1)} %pad_maximum_fusion.1), channel_id=1, source_target_pairs={{0,1},{1,0},{2,3},{3,2},{4,5},{5,4},{6,7},{7,6},{8,9},{9,8},{10,11... | collective-permute-start | bytes 1572872 | tf_op jit(solution)/shard_map/ppermute | solution.py:28
  53.2 1.4 %copy-start.4 = (f16[1024,1024]{1,0:T(8,128)(2,1)}, f16[1024,1024]{1,0:T(8,128)(2,1)S(1)}, u32[]{:S(2)}) copy-start(f16[1024,1024]{1,0:T(8,128)(2,1)S(1)} %fusion) | copy-start | bytes 6291460
  54.5 6.8 %copy-start.6 = (bf16[19,64,64]{2,1,0:T(8,128)(2,1)S(1)}, bf16[19,64,64]{2,1,0:T(8,128)(2,1)}, u32[]{:S(2)}) copy-start(bf16[19,64,64]{2,1,0:T(8,128)(2,1)} %param.16) | copy-start | bytes 466948
  54.5 7.4 %copy-start.7 = (bf16[4,32768]{1,0:T(4,128)(2,1)S(1)}, bf16[4,32768]{1,0:T(4,128)(2,1)}, u32[]{:S(2)}) copy-start(bf16[4,32768]{1,0:T(4,128)(2,1)} %param.15) | copy-start | bytes 786436
  54.5 7.8 %copy-start.1 = (s32[8,2]{0,1:T(2,128)S(1)}, s32[8,2]{0,1:T(2,128)}, u32[]{:S(2)}) copy-start(s32[8,2]{0,1:T(2,128)} %param.14) | copy-start | bytes 196
  54.5 34.9 %all-to-all-start = ((f16[8,128,1024]{2,1,0:T(8,128)(2,1)}), f16[8,128,1024]{2,1,0:T(8,128)(2,1)S(1)}, u32[]{:S(2)}, u32[]{:S(2)}) async-start(f16[8,128,1024]{2,1,0:T(8,128)(2,1)} %bitcast.51), calls=%async_computation | async-start | bytes 4194304 | tf_op jit(solution)/shard_map/all_to_all | solution.py:136
  64.0 1.9 %copy-start.9 = (f32[1216]{0:T(1024)S(1)}, f32[1216]{0:T(1024)}, u32[]{:S(2)}) copy-start(f32[1216]{0:T(1024)} %param.18) | copy-start | bytes 14596
  65.9 31.3 %copy-start.10 = (s32[4,2]{0,1:T(2,128)S(1)}, s32[4,2]{0,1:T(2,128)}, u32[]{:S(2)}) copy-start(s32[4,2]{0,1:T(2,128)} %param.19) | copy-start | bytes 100
  65.9 31.3 %copy-start.11 = (f32[120]{0:T(128)S(1)}, f32[120]{0:T(128)}, u32[]{:S(2)}) copy-start(f32[120]{0:T(128)} %param.17) | copy-start | bytes 1444
  66.2 42.3 %copy-start.5 = (f32[4,32768]{1,0:T(4,128)S(1)}, f32[4,32768]{1,0:T(4,128)}, u32[]{:S(2)}) copy-start(f32[4,32768]{1,0:T(4,128)} %reshape.63) | copy-start | bytes 1572868
  90.9 17.5 %all-to-all-start.1 = ((f16[32,4,1024]{2,1,0:T(4,128)(2,1)}), f16[32,4,1024]{2,1,0:T(4,128)(2,1)S(1)}, u32[]{:S(2)}, u32[]{:S(2)}) async-start(f16[32,4,1024]{2,1,0:T(4,128)(2,1)} %convert_element_type.48), calls=%async_computation.1 | async-start | bytes 524288 | tf_op jit(solution)/shard_map/all_to_all | solution.py:142

commit v2 on v1

--- a/solution.py
+++ b/solution.py
@@ -51,42 +51,44 @@
     r1 = send(b1, NEIGHBOUR)
     q1 = after(q1, b1)
     q2 = send(q1, RING)
-    x0 = after(x0, q1)
+    a2 = after(a2, q1)
+    a3 = send(a2, RING)
+    b2 = after(b2, a2)
+    b3 = send(b2, RING)
+    x0 = after(x0, b2)
     bx = send(x0, SIBLING)
-
-    a2 = after(a2, x0)
-    a3 = send(a2, RING)
-    b2 = after(b2, a2, bx)
-    b3 = send(b2, RING)
     r2 = send(b2, NEIGHBOUR)
-    q2 = after(q2, b2)
+    q2 = after(q2, x0)
     q3 = send(q2, RING)
-    r1 = after(r1, q2)
+    a3 = after(a3, q2, bx)
+    a4 = send(a3, RING)
+    r1 = after(r1, a3)
     near = stack(b1, a1, r1, q1)
     c1 = send(near, SIBLING)
-
     a3 = after(a3, near)
-    a4 = send(a3, RING)
-    b3 = after(b3, a3, c1)
+    b3 = after(b3, a3)
     r3 = send(b3, NEIGHBOUR)
-    q3 = after(q3, b3)
+    q3 = after(q3, b3, c1)
     q4 = send(q3, RING)
     r2 = after(r2, q3)
     middle = stack(b2, a2, r2, q2)
     c2 = send(middle, SIBLING)
     product = multiply(stack(after(own, middle), b0, x0, bx, a1, b1, q1, r1, c1))
     partial = jnp.pad(product, ((0, 20 * rows), (0, 0)))
-
-    c2 = after(c2, partial)
-    product = multiply(stack(a2, b2, q2, r2, c2))
+    r3 = after(r3, partial)
+    third = stack(b3, a3, r3, q3)
+    c3 = send(third, SIBLING)
+    product = multiply(stack(after(a2, third), b2, q2, r2, c2))
     partial = lax.dynamic_update_slice(partial, product, (12 * rows, 0))
     a4 = after(a4, partial)
-    r3 = after(r3, a4)
-    c3 = send(stack(b3, a3, r3, q3), SIBLING)
-    q4 = after(q4, r3)
-    c4 = send(stack(a4, q4), SIBLING)
-    product = multiply(stack(a3, b3, q3, r3, c3, a4, c4[:rows], q4, c4[rows:]))
-    return lax.dynamic_update_slice(partial, product, (20 * rows, 0))
+    q4 = after(q4, a4)
+    fourth = stack(a4, q4)
+    c4 = send(fourth, SIBLING)
+    product = multiply(stack(after(a3, fourth), b3, q3, r3, c3))
+    partial = lax.dynamic_update_slice(partial, product, (20 * rows, 0))
+    c4 = after(c4, partial)
+    product = multiply(stack(a4, c4[:rows], q4, c4[rows:]))
+    return lax.dynamic_update_slice(partial, product, (28 * rows, 0))
 
 
 def mask_kernel(cd_pairs, block_irrep, ab_blocks, scale):

time: 110 us -> 108 us (0.982)
  waiting for transfers between devices: 42.6 us -> 36.7 us
  starting transfers between devices: 44.2 us -> 47.3 us
    ppermute x21, waiting for transfers between devices: 8.31 us -> 2.27 us  [send(): return lax.ppermute(x, 'mem', perm)]
    ppermute x21, starting transfers between devices: 31.4 us -> 33.5 us  [send(): return lax.ppermute(x, 'mem', perm)]
    dot_general x3 -> x4, matrix products: 9.4 us -> 9.67 us  [multiply(): jnp.dot(rows, ladder_integrals, preferred_element_type=jnp.float32)]
    unnamed x50 -> x52, local copies, waits for them, and re-layouts: 3.92 us -> 3.88 us
  transfers between devices with their start and end apart: 23 -> 23, of which waited for: 9 -> 6; matrix products, arithmetic and copies ran while one was open for 11% -> 14% of each run, Pallas kernels for 1% -> 1%
where the time goes in v2:
time: 108 us; the launch traced here: 107 us
  starting transfers between devices  47.3 us (44%)
  waiting for transfers between devices  36.7 us (34%)
  matrix products  12 us (11%)
  local copies, waits for them, and re-layouts  7.8 us (7%)
  other arithmetic  2.2 us (2%)
    ppermute x21, starting transfers between devices, send(): return lax.ppermute(x, 'mem', perm)  33.5 us
    all_to_all x1, waiting for transfers between devices, local(): lax.all_to_all(partial, ('grp', 'mem'), split_axis=0, concat_axis=0, axis...  23.4 us
    all_to_all x1, waiting for transfers between devices, local(): lax.all_to_all(summed, 'mem', split_axis=0, concat_axis=0)  11 us
    dot_general x4, matrix products, multiply(): jnp.dot(rows, ladder_integrals, preferred_element_type=jnp.float32)  9.67 us
    all_to_all x1, starting transfers between devices, local(): lax.all_to_all(summed, 'mem', split_axis=0, concat_axis=0)  6.99 us
    all_to_all x1, starting transfers between devices, local(): lax.all_to_all(partial, ('grp', 'mem'), split_axis=0, concat_axis=0, axis...  6.78 us
    unnamed x52, local copies, waits for them, and re-layouts  3.88 us
    ppermute x21, waiting for transfers between devices, send(): return lax.ppermute(x, 'mem', perm)  2.27 us
  transfers between devices with their start and end apart: 23, of which 6 were waited for; matrix products, arithmetic and copies ran while one was open for 14% of the time, Pallas kernels for 1%

profile of v2, /device:TPU:1, one launch (start us, length us, event | category | flops | bytes accessed | tf_op | source)
XLA Modules:
  0.0 107.2 jit_solution(10763886275158911941)
XLA Ops:
  0.0 6.4 %collective-permute-start.1 = (bf16[32,4096]{1,0:T(8,128)(2,1)}, bf16[32,4096]{1,0:T(8,128)(2,1)S(1)}, u32[]{:S(2)}, u32[]{:S(2)}) collective-permute-start(bf16[32,4096]{1,0:T(8,128)(2,1)} %param.10), channel_id=1, source_target_pairs={{0,4},{1,29},{2,6},{3,31},{4,8},{5,1},{6,10},{7,3},{8,12},{9,5},{1... | collective-permute-start | bytes 786440 | tf_op jit(solution)/shard_map/ppermute | solution.py:28
  6.4 4.0 %collective-permute-start.5 = (bf16[32,4096]{1,0:T(8,128)(2,1)}, bf16[32,4096]{1,0:T(8,128)(2,1)S(1)}, u32[]{:S(2)}, u32[]{:S(2)}) collective-permute-start(bf16[32,4096]{1,0:T(8,128)(2,1)} %param.10), channel_id=1, source_target_pairs={{0,6},{1,31},{2,4},{3,29},{4,10},{5,3},{6,8},{7,1},{8,14},{9,7},{1... | collective-permute-start | bytes 786440 | tf_op jit(solution)/shard_map/ppermute | solution.py:28
  10.4 0.3 collective-permute-start.8
  10.7 0.7 copy-done
  11.3 0.7 copy-done.2
  12.0 0.7 copy-done.3
  12.7 0.6 shard_map.100
  13.2 1.3 %collective-permute-start.4 = (bf16[32,4096]{1,0:T(8,128)(2,1)S(1)}, bf16[32,4096]{1,0:T(8,128)(2,1)S(1)}, u32[]{:S(2)}, u32[]{:S(2)}) collective-permute-start(bf16[32,4096]{1,0:T(8,128)(2,1)S(1)} %collective-permute-done.1), channel_id=1, source_target_pairs={{0,4},{1,29},{2,6},{3,31},{4,8},{5,1},{6,10},{7,3},{8,12},{9,5},{1... | collective-permute-start | bytes 786440 | tf_op jit(solution)/shard_map/ppermute | solution.py:28
  14.5 0.7 collective-permute-done
  15.3 2.1 %collective-permute-start.3 = (bf16[32,4096]{1,0:T(8,128)(2,1)S(1)}, bf16[32,4096]{1,0:T(8,128)(2,1)S(1)}, u32[]{:S(2)}, u32[]{:S(2)}) collective-permute-start(bf16[32,4096]{1,0:T(8,128)(2,1)S(1)} %collective-permute-done), channel_id=1, source_target_pairs={{0,4},{1,29},{2,6},{3,31},{4,8},{5,1},{6,10},{7,3},{8,12},{9,5},{1... | collective-permute-start | bytes 786440 | tf_op jit(solution)/shard_map/ppermute | solution.py:28
  17.3 1.2 %collective-permute-start.13 = (bf16[32,4096]{1,0:T(8,128)(2,1)S(1)}, bf16[32,4096]{1,0:T(8,128)(2,1)S(1)}, u32[]{:S(2)}, u32[]{:S(2)}) collective-permute-start(bf16[32,4096]{1,0:T(8,128)(2,1)S(1)} %collective-permute-done), channel_id=1, source_target_pairs={{0,2},{1,3},{2,0},{3,1},{4,6},{5,7},{6,4},{7,5},{8,10},{9,11},{10,... | collective-permute-start | bytes 786440 | tf_op jit(solution)/shard_map/ppermute | solution.py:28
  18.6 2.6 %collective-permute-start.7 = (bf16[32,4096]{1,0:T(8,128)(2,1)S(1)}, bf16[32,4096]{1,0:T(8,128)(2,1)S(1)}, u32[]{:S(2)}, u32[]{:S(2)}) collective-permute-start(bf16[32,4096]{1,0:T(8,128)(2,1)S(1)} %collective-permute-done.5), channel_id=1, source_target_pairs={{0,4},{1,29},{2,6},{3,31},{4,8},{5,1},{6,10},{7,3},{8,12},{9,5},{1... | collective-permute-start | bytes 786440 | tf_op jit(solution)/shard_map/ppermute | solution.py:28
  21.2 0.0 copy-start.9
  21.2 0.3 collective-permute-start.11
  21.5 0.2 collective-permute-done.3
  21.6 2.6 %collective-permute-start.10 = (bf16[32,4096]{1,0:T(8,128)(2,1)S(1)}, bf16[32,4096]{1,0:T(8,128)(2,1)S(1)}, u32[]{:S(2)}, u32[]{:S(2)}) collective-permute-start(bf16[32,4096]{1,0:T(8,128)(2,1)S(1)} %collective-permute-done.3), channel_id=1, source_target_pairs={{0,4},{1,29},{2,6},{3,31},{4,8},{5,1},{6,10},{7,3},{8,12},{9,5},{1... | collective-permute-start | bytes 786440 | tf_op jit(solution)/shard_map/ppermute | solution.py:28
  24.3 1.2 %collective-permute-start.6 = (bf16[32,4096]{1,0:T(8,128)(2,1)S(1)}, bf16[32,4096]{1,0:T(8,128)(2,1)S(1)}, u32[]{:S(2)}, u32[]{:S(2)}) collective-permute-start(bf16[32,4096]{1,0:T(8,128)(2,1)S(1)} %collective-permute-done.3), channel_id=1, source_target_pairs={{0,2},{1,3},{2,0},{3,1},{4,6},{5,7},{6,4},{7,5},{8,10},{9,11},{10,... | collective-permute-start | bytes 786440 | tf_op jit(solution)/shard_map/ppermute | solution.py:28
  25.5 1.6 %collective-permute-start.12 = (bf16[32,4096]{1,0:T(8,128)(2,1)S(1)}, bf16[32,4096]{1,0:T(8,128)(2,1)S(1)}, u32[]{:S(2)}, u32[]{:S(2)}) collective-permute-start(bf16[32,4096]{1,0:T(8,128)(2,1)S(1)} %collective-permute-done.8), channel_id=1, source_target_pairs={{0,1},{1,0},{2,3},{3,2},{4,5},{5,4},{6,7},{7,6},{8,9},{9,8},{10,11... | collective-permute-start | bytes 786440 | tf_op jit(solution)/shard_map/ppermute | solution.py:28
  27.1 1.1 %collective-permute-done.12 = bf16[32,4096]{1,0:T(8,128)(2,1)S(1)} collective-permute-done((bf16[32,4096]{1,0:T(8,128)(2,1)S(1)}, bf16[32,4096]{1,0:T(8,128)(2,1)S(1)}, u32[]{:S(2)}, u32[]{:S(2)}) %collective-permute-start.12) | collective-permute-done | bytes 262176 | tf_op jit(solution)/shard_map/ppermute | solution.py:28
  28.3 2.3 %collective-permute-start.9 = (bf16[32,4096]{1,0:T(8,128)(2,1)S(1)}, bf16[32,4096]{1,0:T(8,128)(2,1)S(1)}, u32[]{:S(2)}, u32[]{:S(2)}) collective-permute-start(bf16[32,4096]{1,0:T(8,128)(2,1)S(1)} %collective-permute-done.7), channel_id=1, source_target_pairs={{0,4},{1,29},{2,6},{3,31},{4,8},{5,1},{6,10},{7,3},{8,12},{9,5},{1... | collective-permute-start | bytes 786440 | tf_op jit(solution)/shard_map/ppermute | solution.py:28
  30.6 0.1 collective-permute-start.14
  30.7 1.7 %collective-permute-start.17 = (bf16[32,4096]{1,0:T(8,128)(2,1)S(1)}, bf16[32,4096]{1,0:T(8,128)(2,1)S(1)}, u32[]{:S(2)}, u32[]{:S(2)}) collective-permute-start(bf16[32,4096]{1,0:T(8,128)(2,1)S(1)} %collective-permute-done.11), channel_id=1, source_target_pairs={{0,4},{1,29},{2,6},{3,31},{4,8},{5,1},{6,10},{7,3},{8,12},{9,5},{1... | collective-permute-start | bytes 786440 | tf_op jit(solution)/shard_map/ppermute | solution.py:28
  32.4 1.2 %collective-permute-start.15 = (bf16[32,4096]{1,0:T(8,128)(2,1)S(1)}, bf16[32,4096]{1,0:T(8,128)(2,1)S(1)}, u32[]{:S(2)}, u32[]{:S(2)}) collective-permute-start(bf16[32,4096]{1,0:T(8,128)(2,1)S(1)} %collective-permute-done.10), channel_id=1, source_target_pairs={{0,2},{1,3},{2,0},{3,1},{4,6},{5,7},{6,4},{7,5},{8,10},{9,11},{10,... | collective-permute-start | bytes 786440 | tf_op jit(solution)/shard_map/ppermute | solution.py:28
  33.7 0.2 collective-permute-done.9
  33.9 2.5 %collective-permute-start.16 = (bf16[128,4096]{1,0:T(8,128)(2,1)S(1)}, bf16[128,4096]{1,0:T(8,128)(2,1)S(1)}, u32[]{:S(2)}, u32[]{:S(2)}) collective-permute-start(bf16[128,4096]{1,0:T(8,128)(2,1)S(1)} %constant_dynamic-update-slice_fusion.4), channel_id=1, source_target_pairs={{0,1},{1,0},{2,3},{3,2},{4,5},{5,4},{6,7},{7,6},{8,9},{9,8},{10,11... | collective-permute-start | bytes 3145736 | tf_op jit(solution)/shard_map/ppermute | solution.py:28
  36.4 1.6 %collective-permute-start.18 = (bf16[32,4096]{1,0:T(8,128)(2,1)S(1)}, bf16[32,4096]{1,0:T(8,128)(2,1)S(1)}, u32[]{:S(2)}, u32[]{:S(2)}) collective-permute-start(bf16[32,4096]{1,0:T(8,128)(2,1)S(1)} %collective-permute-done.9), channel_id=1, source_target_pairs={{0,4},{1,29},{2,6},{3,31},{4,8},{5,1},{6,10},{7,3},{8,12},{9,5},{1... | collective-permute-start | bytes 786440 | tf_op jit(solution)/shard_map/ppermute | solution.py:28
  38.2 0.1 constant_dynamic-update-slice_fusion.8
  38.3 3.5 %multiply_convert_fusion = f16[384,1024]{1,0:T(8,128)(2,1)S(1)} fusion(bf16[384,4096]{1,0:T(8,128)(2,1)S(1)} %constant_dynamic-update-slice_fusion.8, bf16[4096,1024]{1,0:T(8,128)(2,1)S(1)} %copy-done.4, f32[]{:T(128)S(1)} %bitcast.50), kind=kOutput, calls=%fused_computation.1 | convolution fusion | flops 3222011904 | bytes 12320772 | tf_op jit(solution)/shard_map/dot_general | solution.py:133
  41.8 0.3 pad.4
  42.1 0.1 collective-permute-start.19
  42.4 0.1 constant_dynamic-update-slice_fusion.21
  42.5 2.4 %fusion.2 = f16[1024,1024]{1,0:T(8,128)(2,1)S(1)} fusion(f16[1024,1024]{1,0:T(8,128)(2,1)S(1)} %pad.4, bf16[256,4096]{1,0:T(8,128)(2,1)S(1)} %constant_dynamic-update-slice_fusion.21, bf16[4096,1024]{1,0:T(8,128)(2,1)S(1)} %copy-done.4, f32[]{:T(128)S(1)} %bitcast.51), kind=kOutput, calls=%fused_computation.8 | convolution fusion | flops 2148007936 | bytes 11010560 | tf_op jit(solution)/shard_map/dot_general | solution.py:133
  44.9 0.6 collective-permute-start.20
  45.6 0.1 constant_dynamic-update-slice_fusion.28
  45.7 2.4 %fusion.4 = f16[1024,1024]{1,0:T(8,128)(2,1)S(1)} fusion(f16[1024,1024]{1,0:T(8,128)(2,1)S(1)} %fusion.2, bf16[256,4096]{1,0:T(8,128)(2,1)S(1)} %constant_dynamic-update-slice_fusion.28, bf16[4096,1024]{1,0:T(8,128)(2,1)S(1)} %copy-done.4, f32[]{:T(128)S(1)} %bitcast.52), kind=kOutput, calls=%fused_computation.10 | convolution fusion | flops 2148007936 | bytes 11010560 | tf_op jit(solution)/shard_map/dot_general | solution.py:133
  48.2 0.1 pad_maximum_fusion
  48.2 1.4 %fusion.6 = f16[1024,1024]{1,0:T(8,128)(2,1)S(1)} fusion(f16[1024,1024]{1,0:T(8,128)(2,1)S(1)} %fusion.4, bf16[128,4096]{1,0:T(8,128)(2,1)S(1)} %pad_maximum_fusion, bf16[4096,1024]{1,0:T(8,128)(2,1)S(1)} %copy-done.4, f32[]{:T(128)S(1)} %bitcast.53), kind=kOutput, calls=%fused_computation.13 | convolution fusion | flops 1074003968 | bytes 9699840 | tf_op jit(solution)/shard_map/dot_general | solution.py:133
  49.6 1.3 %copy-done.5 = f16[1024,1024]{1,0:T(8,128)(2,1)} copy-done((f16[1024,1024]{1,0:T(8,128)(2,1)}, f16[1024,1024]{1,0:T(8,128)(2,1)S(1)}, u32[]{:S(2)}) %copy-start.5) | copy-done | bytes 2097176
  51.0 6.8 %all-to-all-start = ((f16[8,128,1024]{2,1,0:T(8,128)(2,1)}), f16[8,128,1024]{2,1,0:T(8,128)(2,1)S(1)}, u32[]{:S(2)}, u32[]{:S(2)}) async-start(f16[8,128,1024]{2,1,0:T(8,128)(2,1)} %bitcast.54), calls=%async_computation | async-start | bytes 4194304 | tf_op jit(solution)/shard_map/all_to_all | solution.py:138
  57.8 0.3 reshape.61
  58.1 0.3 dot_general.39
  58.4 0.4 reshape.62
  58.8 0.1 fusion.14
  58.9 0.5 convolution_bitcast_fusion.3
  59.4 0.5 convolution_bitcast_fusion.2
  59.9 0.6 convolution_bitcast_fusion.1
  60.4 0.6 fusion
  61.0 0.1 copy.35
  61.1 1.2 %reshape.63 = f32[4,32768]{1,0:T(4,128)} reshape(f32[4,8,64,64]{3,2,1,0:T(8,128)S(1)} %copy.35) | data formatting | bytes 1048576 | tf_op jit(solution)/shard_map/reshape | solution.py:176
  62.3 0.1 reshape.64
  62.4 0.1 fusion.16
  62.5 0.1 fusion.19
  62.7 23.4 %all-to-all-done = f16[8,128,1024]{2,1,0:T(8,128)(2,1)S(1)} async-done(((f16[8,128,1024]{2,1,0:T(8,128)(2,1)}), f16[8,128,1024]{2,1,0:T(8,128)(2,1)S(1)}, u32[]{:S(2)}, u32[]{:S(2)}) %all-to-all-start) | async-done | bytes 2097184 | tf_op jit(solution)/shard_map/all_to_all | solution.py:138
  86.1 0.5 convert_reduce_fusion
  86.6 0.0 copy-start.11
  86.6 0.0 copy-start.12
  86.7 0.8 convert_element_type.52
  87.5 7.0 %all-to-all-start.1 = ((f16[32,4,1024]{2,1,0:T(4,128)(2,1)}), f16[32,4,1024]{2,1,0:T(4,128)(2,1)S(1)}, u32[]{:S(2)}, u32[]{:S(2)}) async-start(f16[32,4,1024]{2,1,0:T(4,128)(2,1)} %convert_element_type.52), calls=%async_computation.1 | async-start | bytes 524288 | tf_op jit(solution)/shard_map/all_to_all | solution.py:144
  94.5 0.1 broadcast_add_fusion
  94.7 0.1 add.54
  94.8 0.2 select_reduce_fusion
  95.0 11.0 %all-to-all-done.1 = f16[32,4,1024]{2,1,0:T(4,128)(2,1)S(1)} async-done(((f16[32,4,1024]{2,1,0:T(4,128)(2,1)}), f16[32,4,1024]{2,1,0:T(4,128)(2,1)S(1)}, u32[]{:S(2)}, u32[]{:S(2)}) %all-to-all-start.1) | async-done | bytes 262176 | tf_op jit(solution)/shard_map/all_to_all | solution.py:144
  106.0 0.1 convert_multiply_fusion
  106.1 1.0 subtract_divide_fusion
  (72 shorter events, 0.8 us)
Async XLA Ops:
  0.0 13.2 %collective-permute-start.1 = (bf16[32,4096]{1,0:T(8,128)(2,1)}, bf16[32,4096]{1,0:T(8,128)(2,1)S(1)}, u32[]{:S(2)}, u32[]{:S(2)}) collective-permute-start(bf16[32,4096]{1,0:T(8,128)(2,1)} %param.10), channel_id=1, source_target_pairs={{0,4},{1,29},{2,6},{3,31},{4,8},{5,1},{6,10},{7,3},{8,12},{9,5},{1... | collective-permute-start | bytes 786440 | tf_op jit(solution)/shard_map/ppermute | solution.py:28
  6.4 8.1 %collective-permute-start.2 = (bf16[32,4096]{1,0:T(8,128)(2,1)}, bf16[32,4096]{1,0:T(8,128)(2,1)S(1)}, u32[]{:S(2)}, u32[]{:S(2)}) collective-permute-start(bf16[32,4096]{1,0:T(8,128)(2,1)} %param.10), channel_id=1, source_target_pairs={{0,1},{1,0},{2,3},{3,2},{4,5},{5,4},{6,7},{7,6},{8,9},{9,8},{10,11... | collective-permute-start | bytes 786440 | tf_op jit(solution)/shard_map/ppermute | solution.py:28
  6.4 8.8 %collective-permute-start = (bf16[32,4096]{1,0:T(8,128)(2,1)}, bf16[32,4096]{1,0:T(8,128)(2,1)S(1)}, u32[]{:S(2)}, u32[]{:S(2)}) collective-permute-start(bf16[32,4096]{1,0:T(8,128)(2,1)} %param.10), channel_id=1, source_target_pairs={{0,29},{1,4},{2,31},{3,6},{4,1},{5,8},{6,3},{7,10},{8,5},{9,12},{1... | collective-permute-start | bytes 786440 | tf_op jit(solution)/shard_map/ppermute | solution.py:28
  6.4 12.2 %collective-permute-start.5 = (bf16[32,4096]{1,0:T(8,128)(2,1)}, bf16[32,4096]{1,0:T(8,128)(2,1)S(1)}, u32[]{:S(2)}, u32[]{:S(2)}) collective-permute-start(bf16[32,4096]{1,0:T(8,128)(2,1)} %param.10), channel_id=1, source_target_pairs={{0,6},{1,31},{2,4},{3,29},{4,10},{5,3},{6,8},{7,1},{8,14},{9,7},{1... | collective-permute-start | bytes 786440 | tf_op jit(solution)/shard_map/ppermute | solution.py:28
  10.4 13.9 %collective-permute-start.8 = (bf16[32,4096]{1,0:T(8,128)(2,1)}, bf16[32,4096]{1,0:T(8,128)(2,1)S(1)}, u32[]{:S(2)}, u32[]{:S(2)}) collective-permute-start(bf16[32,4096]{1,0:T(8,128)(2,1)} %param.10), channel_id=1, source_target_pairs={{0,2},{1,3},{2,0},{3,1},{4,6},{5,7},{6,4},{7,5},{8,10},{9,11},{10,... | collective-permute-start | bytes 786440 | tf_op jit(solution)/shard_map/ppermute | solution.py:28
  10.7 0.7 copy-start
  11.3 0.7 copy-start.2
  12.0 0.7 copy-start.3
  13.2 7.9 %collective-permute-start.4 = (bf16[32,4096]{1,0:T(8,128)(2,1)S(1)}, bf16[32,4096]{1,0:T(8,128)(2,1)S(1)}, u32[]{:S(2)}, u32[]{:S(2)}) collective-permute-start(bf16[32,4096]{1,0:T(8,128)(2,1)S(1)} %collective-permute-done.1), channel_id=1, source_target_pairs={{0,4},{1,29},{2,6},{3,31},{4,8},{5,1},{6,10},{7,3},{8,12},{9,5},{1... | collective-permute-start | bytes 786440 | tf_op jit(solution)/shard_map/ppermute | solution.py:28
  15.3 6.4 %collective-permute-start.3 = (bf16[32,4096]{1,0:T(8,128)(2,1)S(1)}, bf16[32,4096]{1,0:T(8,128)(2,1)S(1)}, u32[]{:S(2)}, u32[]{:S(2)}) collective-permute-start(bf16[32,4096]{1,0:T(8,128)(2,1)S(1)} %collective-permute-done), channel_id=1, source_target_pairs={{0,4},{1,29},{2,6},{3,31},{4,8},{5,1},{6,10},{7,3},{8,12},{9,5},{1... | collective-permute-start | bytes 786440 | tf_op jit(solution)/shard_map/ppermute | solution.py:28
  17.3 13.2 %collective-permute-start.13 = (bf16[32,4096]{1,0:T(8,128)(2,1)S(1)}, bf16[32,4096]{1,0:T(8,128)(2,1)S(1)}, u32[]{:S(2)}, u32[]{:S(2)}) collective-permute-start(bf16[32,4096]{1,0:T(8,128)(2,1)S(1)} %collective-permute-done), channel_id=1, source_target_pairs={{0,2},{1,3},{2,0},{3,1},{4,6},{5,7},{6,4},{7,5},{8,10},{9,11},{10,... | collective-permute-start | bytes 786440 | tf_op jit(solution)/shard_map/ppermute | solution.py:28
  18.6 6.9 %collective-permute-start.7 = (bf16[32,4096]{1,0:T(8,128)(2,1)S(1)}, bf16[32,4096]{1,0:T(8,128)(2,1)S(1)}, u32[]{:S(2)}, u32[]{:S(2)}) collective-permute-start(bf16[32,4096]{1,0:T(8,128)(2,1)S(1)} %collective-permute-done.5), channel_id=1, source_target_pairs={{0,4},{1,29},{2,6},{3,31},{4,8},{5,1},{6,10},{7,3},{8,12},{9,5},{1... | collective-permute-start | bytes 786440 | tf_op jit(solution)/shard_map/ppermute | solution.py:28
  21.2 16.8 %copy-start.9 = (bf16[32,4096]{1,0:T(8,128)(2,1)S(1)}, bf16[32,4096]{1,0:T(8,128)(2,1)}, u32[]{:S(2)}) copy-start(bf16[32,4096]{1,0:T(8,128)(2,1)} %param.10) | copy-start | bytes 786436
  21.2 9.4 %collective-permute-start.11 = (bf16[32,4096]{1,0:T(8,128)(2,1)S(1)}, bf16[32,4096]{1,0:T(8,128)(2,1)S(1)}, u32[]{:S(2)}, u32[]{:S(2)}) collective-permute-start(bf16[32,4096]{1,0:T(8,128)(2,1)S(1)} %collective-permute-done.4), channel_id=1, source_target_pairs={{0,4},{1,29},{2,6},{3,31},{4,8},{5,1},{6,10},{7,3},{8,12},{9,5},{1... | collective-permute-start | bytes 786440 | tf_op jit(solution)/shard_map/ppermute | solution.py:28
  21.6 10.8 %collective-permute-start.10 = (bf16[32,4096]{1,0:T(8,128)(2,1)S(1)}, bf16[32,4096]{1,0:T(8,128)(2,1)S(1)}, u32[]{:S(2)}, u32[]{:S(2)}) collective-permute-start(bf16[32,4096]{1,0:T(8,128)(2,1)S(1)} %collective-permute-done.3), channel_id=1, source_target_pairs={{0,4},{1,29},{2,6},{3,31},{4,8},{5,1},{6,10},{7,3},{8,12},{9,5},{1... | collective-permute-start | bytes 786440 | tf_op jit(solution)/shard_map/ppermute | solution.py:28
  24.3 9.6 %collective-permute-start.6 = (bf16[32,4096]{1,0:T(8,128)(2,1)S(1)}, bf16[32,4096]{1,0:T(8,128)(2,1)S(1)}, u32[]{:S(2)}, u32[]{:S(2)}) collective-permute-start(bf16[32,4096]{1,0:T(8,128)(2,1)S(1)} %collective-permute-done.3), channel_id=1, source_target_pairs={{0,2},{1,3},{2,0},{3,1},{4,6},{5,7},{6,4},{7,5},{8,10},{9,11},{10,... | collective-permute-start | bytes 786440 | tf_op jit(solution)/shard_map/ppermute | solution.py:28
  25.5 2.8 %collective-permute-start.12 = (bf16[32,4096]{1,0:T(8,128)(2,1)S(1)}, bf16[32,4096]{1,0:T(8,128)(2,1)S(1)}, u32[]{:S(2)}, u32[]{:S(2)}) collective-permute-start(bf16[32,4096]{1,0:T(8,128)(2,1)S(1)} %collective-permute-done.8), channel_id=1, source_target_pairs={{0,1},{1,0},{2,3},{3,2},{4,5},{5,4},{6,7},{7,6},{8,9},{9,8},{10,11... | collective-permute-start | bytes 786440 | tf_op jit(solution)/shard_map/ppermute | solution.py:28
  28.3 5.6 %collective-permute-start.9 = (bf16[32,4096]{1,0:T(8,128)(2,1)S(1)}, bf16[32,4096]{1,0:T(8,128)(2,1)S(1)}, u32[]{:S(2)}, u32[]{:S(2)}) collective-permute-start(bf16[32,4096]{1,0:T(8,128)(2,1)S(1)} %collective-permute-done.7), channel_id=1, source_target_pairs={{0,4},{1,29},{2,6},{3,31},{4,8},{5,1},{6,10},{7,3},{8,12},{9,5},{1... | collective-permute-start | bytes 786440 | tf_op jit(solution)/shard_map/ppermute | solution.py:28
  30.6 3.3 %collective-permute-start.14 = (bf16[128,4096]{1,0:T(8,128)(2,1)S(1)}, bf16[128,4096]{1,0:T(8,128)(2,1)S(1)}, u32[]{:S(2)}, u32[]{:S(2)}) collective-permute-start(bf16[128,4096]{1,0:T(8,128)(2,1)S(1)} %constant_dynamic-update-slice_fusion), channel_id=1, source_target_pairs={{0,1},{1,0},{2,3},{3,2},{4,5},{5,4},{6,7},{7,6},{8,9},{9,8},{10,11... | collective-permute-start | bytes 3145736 | tf_op jit(solution)/shard_map/ppermute | solution.py:28
  30.7 14.1 %collective-permute-start.17 = (bf16[32,4096]{1,0:T(8,128)(2,1)S(1)}, bf16[32,4096]{1,0:T(8,128)(2,1)S(1)}, u32[]{:S(2)}, u32[]{:S(2)}) collective-permute-start(bf16[32,4096]{1,0:T(8,128)(2,1)S(1)} %collective-permute-done.11), channel_id=1, source_target_pairs={{0,4},{1,29},{2,6},{3,31},{4,8},{5,1},{6,10},{7,3},{8,12},{9,5},{1... | collective-permute-start | bytes 786440 | tf_op jit(solution)/shard_map/ppermute | solution.py:28
  32.4 9.7 %collective-permute-start.15 = (bf16[32,4096]{1,0:T(8,128)(2,1)S(1)}, bf16[32,4096]{1,0:T(8,128)(2,1)S(1)}, u32[]{:S(2)}, u32[]{:S(2)}) collective-permute-start(bf16[32,4096]{1,0:T(8,128)(2,1)S(1)} %collective-permute-done.10), channel_id=1, source_target_pairs={{0,2},{1,3},{2,0},{3,1},{4,6},{5,7},{6,4},{7,5},{8,10},{9,11},{10,... | collective-permute-start | bytes 786440 | tf_op jit(solution)/shard_map/ppermute | solution.py:28
  33.6 4.6 %copy-start.4 = (bf16[4096,1024]{1,0:T(8,128)(2,1)S(1)}, bf16[4096,1024]{1,0:T(8,128)(2,1)}, u32[]{:S(2)}) copy-start(bf16[4096,1024]{1,0:T(8,128)(2,1)} %param.11) | copy-start | bytes 25165828
  33.9 8.4 %collective-permute-start.16 = (bf16[128,4096]{1,0:T(8,128)(2,1)S(1)}, bf16[128,4096]{1,0:T(8,128)(2,1)S(1)}, u32[]{:S(2)}, u32[]{:S(2)}) collective-permute-start(bf16[128,4096]{1,0:T(8,128)(2,1)S(1)} %constant_dynamic-update-slice_fusion.4), channel_id=1, source_target_pairs={{0,1},{1,0},{2,3},{3,2},{4,5},{5,4},{6,7},{7,6},{8,9},{9,8},{10,11... | collective-permute-start | bytes 3145736 | tf_op jit(solution)/shard_map/ppermute | solution.py:28
  36.4 8.5 %collective-permute-start.18 = (bf16[32,4096]{1,0:T(8,128)(2,1)S(1)}, bf16[32,4096]{1,0:T(8,128)(2,1)S(1)}, u32[]{:S(2)}, u32[]{:S(2)}) collective-permute-start(bf16[32,4096]{1,0:T(8,128)(2,1)S(1)} %collective-permute-done.9), channel_id=1, source_target_pairs={{0,4},{1,29},{2,6},{3,31},{4,8},{5,1},{6,10},{7,3},{8,12},{9,5},{1... | collective-permute-start | bytes 786440 | tf_op jit(solution)/shard_map/ppermute | solution.py:28
  42.1 3.5 %collective-permute-start.19 = (bf16[128,4096]{1,0:T(8,128)(2,1)S(1)}, bf16[128,4096]{1,0:T(8,128)(2,1)S(1)}, u32[]{:S(2)}, u32[]{:S(2)}) collective-permute-start(bf16[128,4096]{1,0:T(8,128)(2,1)S(1)} %constant_dynamic-update-slice_fusion.17), channel_id=1, source_target_pairs={{0,1},{1,0},{2,3},{3,2},{4,5},{5,4},{6,7},{7,6},{8,9},{9,8},{10,11... | collective-permute-start | bytes 3145736 | tf_op jit(solution)/shard_map/ppermute | solution.py:28
  44.9 3.2 %collective-permute-start.20 = (bf16[64,4096]{1,0:T(8,128)(2,1)S(1)}, bf16[64,4096]{1,0:T(8,128)(2,1)S(1)}, u32[]{:S(2)}, u32[]{:S(2)}) collective-permute-start(bf16[64,4096]{1,0:T(8,128)(2,1)S(1)} %constant_dynamic-update-slice_fusion.26), channel_id=1, source_target_pairs={{0,1},{1,0},{2,3},{3,2},{4,5},{5,4},{6,7},{7,6},{8,9},{9,8},{10,11... | collective-permute-start | bytes 1572872 | tf_op jit(solution)/shard_map/ppermute | solution.py:28
  49.6 1.4 %copy-start.5 = (f16[1024,1024]{1,0:T(8,128)(2,1)}, f16[1024,1024]{1,0:T(8,128)(2,1)S(1)}, u32[]{:S(2)}) copy-start(f16[1024,1024]{1,0:T(8,128)(2,1)S(1)} %fusion.6) | copy-start | bytes 6291460
  51.0 6.8 %copy-start.7 = (bf16[19,64,64]{2,1,0:T(8,128)(2,1)S(1)}, bf16[19,64,64]{2,1,0:T(8,128)(2,1)}, u32[]{:S(2)}) copy-start(bf16[19,64,64]{2,1,0:T(8,128)(2,1)} %param.16) | copy-start | bytes 466948
  51.0 7.4 %copy-start.8 = (bf16[4,32768]{1,0:T(4,128)(2,1)S(1)}, bf16[4,32768]{1,0:T(4,128)(2,1)}, u32[]{:S(2)}) copy-start(bf16[4,32768]{1,0:T(4,128)(2,1)} %param.15) | copy-start | bytes 786436
  51.0 7.8 %copy-start.1 = (s32[8,2]{0,1:T(2,128)S(1)}, s32[8,2]{0,1:T(2,128)}, u32[]{:S(2)}) copy-start(s32[8,2]{0,1:T(2,128)} %param.14) | copy-start | bytes 196
  51.0 35.1 %all-to-all-start = ((f16[8,128,1024]{2,1,0:T(8,128)(2,1)}), f16[8,128,1024]{2,1,0:T(8,128)(2,1)S(1)}, u32[]{:S(2)}, u32[]{:S(2)}) async-start(f16[8,128,1024]{2,1,0:T(8,128)(2,1)} %bitcast.54), calls=%async_computation | async-start | bytes 4194304 | tf_op jit(solution)/shard_map/all_to_all | solution.py:138
  61.0 1.3 %copy-start.10 = (f32[1216]{0:T(1024)S(1)}, f32[1216]{0:T(1024)}, u32[]{:S(2)}) copy-start(f32[1216]{0:T(1024)} %param.18) | copy-start | bytes 14596
  86.6 8.2 %copy-start.11 = (s32[4,2]{0,1:T(2,128)S(1)}, s32[4,2]{0,1:T(2,128)}, u32[]{:S(2)}) copy-start(s32[4,2]{0,1:T(2,128)} %param.19) | copy-start | bytes 100
  86.6 8.2 %copy-start.12 = (f32[120]{0:T(128)S(1)}, f32[120]{0:T(128)}, u32[]{:S(2)}) copy-start(f32[120]{0:T(128)} %param.17) | copy-start | bytes 1444
  86.6 19.5 %copy-start.6 = (f32[4,32768]{1,0:T(4,128)S(1)}, f32[4,32768]{1,0:T(4,128)}, u32[]{:S(2)}) copy-start(f32[4,32768]{1,0:T(4,128)} %reshape.63) | copy-start | bytes 1572868
  87.5 18.4 %all-to-all-start.1 = ((f16[32,4,1024]{2,1,0:T(4,128)(2,1)}), f16[32,4,1024]{2,1,0:T(4,128)(2,1)S(1)}, u32[]{:S(2)}, u32[]{:S(2)}) async-start(f16[32,4,1024]{2,1,0:T(4,128)(2,1)} %convert_element_type.52), calls=%async_computation.1 | async-start | bytes 524288 | tf_op jit(solution)/shard_map/all_to_all | solution.py:144

commit v3 on v2

--- a/solution.py
+++ b/solution.py
@@ -141,8 +141,6 @@
     summed = jnp.where(x_lo == 1, summed[::-1], summed)
     summed = jnp.where(core == 1, summed[:, ::-1], summed)
     summed = summed.reshape(MEM, local_rows, col_count).astype(jnp.float16)
-    ladder = lax.all_to_all(summed, "mem", split_axis=0, concat_axis=0).astype(jnp.float32) * (1.0 / 32.0)
-
     out_pairs = ab_blocks.shape[0]
     left_select = out_onehot[:, 0, :].astype(jnp.float32)
     right_select = out_onehot[:, 1, :].astype(jnp.float32)
@@ -175,6 +173,8 @@
     width = out_pairs * pair_width
     dressed = dressed.reshape(local_rows, width)
     denominator = denominator.reshape(local_rows, width)
+    summed, dressed, denominator = lax.optimization_barrier((summed, dressed, denominator))
+    ladder = lax.all_to_all(summed, "mem", split_axis=0, concat_axis=0).astype(jnp.float32) * (1.0 / 32.0)
     ladder = ladder.transpose(1, 0, 2).reshape(local_rows, width)
     return (ladder + dressed) / denominator
 

time: 108 us -> 108 us (level)
  blocking collectives: 0 us -> 19 us
  starting transfers between devices: 47.3 us -> 34.9 us
  waiting for transfers between devices: 36.7 us -> 28.1 us
  other arithmetic: 2.2 us -> 4.47 us
    all_to_all x0 -> x1, blocking collectives: none -> 19 us  [local(): lax.all_to_all(summed, 'mem', split_axis=0, concat_axis=0)]
    all_to_all x1 -> x0, waiting for transfers between devices: 11 us -> none  [local(): lax.all_to_all(summed, 'mem', split_axis=0, concat_axis=0)]
    all_to_all x1 -> x0, starting transfers between devices: 6.99 us -> none  [local(): lax.all_to_all(summed, 'mem', split_axis=0, concat_axis=0)]
    ppermute x21, starting transfers between devices: 33.5 us -> 28.3 us  [send(): return lax.ppermute(x, 'mem', perm)]
    ppermute x21, waiting for transfers between devices: 2.27 us -> 5.29 us  [send(): return lax.ppermute(x, 'mem', perm)]
    unnamed x52 -> x46, local copies, waits for them, and re-layouts: 3.88 us -> 3.84 us
  transfers between devices with their start and end apart: 23 -> 22, of which waited for: 6 -> 6; matrix products, arithmetic and copies ran while one was open for 14% -> 16% of each run, Pallas kernels for 1% -> 1%
where the time goes in v3:
time: 108 us; the launch traced here: 107 us
  starting transfers between devices  34.9 us (32%)
  waiting for transfers between devices  28.1 us (26%)
  blocking collectives  19 us (18%)
  matrix products  12 us (11%)
  local copies, waits for them, and re-layouts  7.78 us (7%)
  other arithmetic  4.47 us (4%)
    ppermute x21, starting transfers between devices, send(): return lax.ppermute(x, 'mem', perm)  28.3 us
    all_to_all x1, waiting for transfers between devices, local(): lax.all_to_all(partial, ('grp', 'mem'), split_axis=0, concat_axis=0, axis...  22.8 us
    all_to_all x1, blocking collectives, local(): lax.all_to_all(summed, 'mem', split_axis=0, concat_axis=0)  19 us
    dot_general x4, matrix products, multiply(): jnp.dot(rows, ladder_integrals, preferred_element_type=jnp.float32)  9.66 us
    all_to_all x1, starting transfers between devices, local(): lax.all_to_all(partial, ('grp', 'mem'), split_axis=0, concat_axis=0, axis...  6.56 us
    ppermute x21, waiting for transfers between devices, send(): return lax.ppermute(x, 'mem', perm)  5.29 us
    unnamed x46, local copies, waits for them, and re-layouts  3.84 us
  transfers between devices with their start and end apart: 22, of which 6 were waited for; matrix products, arithmetic and copies ran while one was open for 16% of the time, Pallas kernels for 1%

profile of v3, /device:TPU:1, one launch (start us, length us, event | category | flops | bytes accessed | tf_op | source)
XLA Modules:
  0.0 107.3 jit_solution(13704919686918719957)
XLA Ops:
  0.0 6.4 %collective-permute-start.1 = (bf16[32,4096]{1,0:T(8,128)(2,1)}, bf16[32,4096]{1,0:T(8,128)(2,1)S(1)}, u32[]{:S(2)}, u32[]{:S(2)}) collective-permute-start(bf16[32,4096]{1,0:T(8,128)(2,1)} %param.10), channel_id=1, source_target_pairs={{0,4},{1,29},{2,6},{3,31},{4,8},{5,1},{6,10},{7,3},{8,12},{9,5},{1... | collective-permute-start | bytes 786440 | tf_op jit(solution)/shard_map/ppermute | solution.py:28
  6.4 4.0 %collective-permute-start.5 = (bf16[32,4096]{1,0:T(8,128)(2,1)}, bf16[32,4096]{1,0:T(8,128)(2,1)S(1)}, u32[]{:S(2)}, u32[]{:S(2)}) collective-permute-start(bf16[32,4096]{1,0:T(8,128)(2,1)} %param.10), channel_id=1, source_target_pairs={{0,6},{1,31},{2,4},{3,29},{4,10},{5,3},{6,8},{7,1},{8,14},{9,7},{1... | collective-permute-start | bytes 786440 | tf_op jit(solution)/shard_map/ppermute | solution.py:28
  10.4 0.3 collective-permute-start.8
  10.7 0.7 fusion.14
  11.4 0.8 reshape.63
  12.2 0.1 fusion.16
  12.3 0.1 fusion.19
  12.4 0.1 broadcast_add_fusion
  12.6 0.9 select_reduce_fusion
  13.4 0.1 add.53
  13.6 0.7 copy-done
  14.2 0.7 copy-done.1
  14.9 0.7 copy-done.2
  15.5 0.6 shard_map.100
  16.1 0.1 collective-permute-start.4
  16.3 1.1 %collective-permute-start.3 = (bf16[32,4096]{1,0:T(8,128)(2,1)S(1)}, bf16[32,4096]{1,0:T(8,128)(2,1)S(1)}, u32[]{:S(2)}, u32[]{:S(2)}) collective-permute-start(bf16[32,4096]{1,0:T(8,128)(2,1)S(1)} %collective-permute-done), channel_id=1, source_target_pairs={{0,4},{1,29},{2,6},{3,31},{4,8},{5,1},{6,10},{7,3},{8,12},{9,5},{1... | collective-permute-start | bytes 786440 | tf_op jit(solution)/shard_map/ppermute | solution.py:28
  17.3 1.2 %collective-permute-start.13 = (bf16[32,4096]{1,0:T(8,128)(2,1)S(1)}, bf16[32,4096]{1,0:T(8,128)(2,1)S(1)}, u32[]{:S(2)}, u32[]{:S(2)}) collective-permute-start(bf16[32,4096]{1,0:T(8,128)(2,1)S(1)} %collective-permute-done), channel_id=1, source_target_pairs={{0,2},{1,3},{2,0},{3,1},{4,6},{5,7},{6,4},{7,5},{8,10},{9,11},{10,... | collective-permute-start | bytes 786440 | tf_op jit(solution)/shard_map/ppermute | solution.py:28
  18.6 2.5 %collective-permute-start.7 = (bf16[32,4096]{1,0:T(8,128)(2,1)S(1)}, bf16[32,4096]{1,0:T(8,128)(2,1)S(1)}, u32[]{:S(2)}, u32[]{:S(2)}) collective-permute-start(bf16[32,4096]{1,0:T(8,128)(2,1)S(1)} %collective-permute-done.5), channel_id=1, source_target_pairs={{0,4},{1,29},{2,6},{3,31},{4,8},{5,1},{6,10},{7,3},{8,12},{9,5},{1... | collective-permute-start | bytes 786440 | tf_op jit(solution)/shard_map/ppermute | solution.py:28
  21.2 0.0 copy-start.9
  21.2 0.6 collective-permute-done.4
  21.7 0.9 collective-permute-start.11
  22.7 1.9 %collective-permute-done.3 = bf16[32,4096]{1,0:T(8,128)(2,1)S(1)} collective-permute-done((bf16[32,4096]{1,0:T(8,128)(2,1)S(1)}, bf16[32,4096]{1,0:T(8,128)(2,1)S(1)}, u32[]{:S(2)}, u32[]{:S(2)}) %collective-permute-start.3) | collective-permute-done | bytes 262176 | tf_op jit(solution)/shard_map/ppermute | solution.py:28
  24.6 0.9 collective-permute-start.10
  25.5 1.2 %collective-permute-start.6 = (bf16[32,4096]{1,0:T(8,128)(2,1)S(1)}, bf16[32,4096]{1,0:T(8,128)(2,1)S(1)}, u32[]{:S(2)}, u32[]{:S(2)}) collective-permute-start(bf16[32,4096]{1,0:T(8,128)(2,1)S(1)} %collective-permute-done.3), channel_id=1, source_target_pairs={{0,2},{1,3},{2,0},{3,1},{4,6},{5,7},{6,4},{7,5},{8,10},{9,11},{10,... | collective-permute-start | bytes 786440 | tf_op jit(solution)/shard_map/ppermute | solution.py:28
  26.7 0.7 collective-permute-done.7
  27.4 1.4 %collective-permute-start.12 = (bf16[32,4096]{1,0:T(8,128)(2,1)S(1)}, bf16[32,4096]{1,0:T(8,128)(2,1)S(1)}, u32[]{:S(2)}, u32[]{:S(2)}) collective-permute-start(bf16[32,4096]{1,0:T(8,128)(2,1)S(1)} %collective-permute-done.8), channel_id=1, source_target_pairs={{0,1},{1,0},{2,3},{3,2},{4,5},{5,4},{6,7},{7,6},{8,9},{9,8},{10,11... | collective-permute-start | bytes 786440 | tf_op jit(solution)/shard_map/ppermute | solution.py:28
  28.8 1.1 %collective-permute-done.12 = bf16[32,4096]{1,0:T(8,128)(2,1)S(1)} collective-permute-done((bf16[32,4096]{1,0:T(8,128)(2,1)S(1)}, bf16[32,4096]{1,0:T(8,128)(2,1)S(1)}, u32[]{:S(2)}, u32[]{:S(2)}) %collective-permute-start.12) | collective-permute-done | bytes 262176 | tf_op jit(solution)/shard_map/ppermute | solution.py:28
  29.9 1.6 %collective-permute-start.9 = (bf16[32,4096]{1,0:T(8,128)(2,1)S(1)}, bf16[32,4096]{1,0:T(8,128)(2,1)S(1)}, u32[]{:S(2)}, u32[]{:S(2)}) collective-permute-start(bf16[32,4096]{1,0:T(8,128)(2,1)S(1)} %collective-permute-done.7), channel_id=1, source_target_pairs={{0,4},{1,29},{2,6},{3,31},{4,8},{5,1},{6,10},{7,3},{8,12},{9,5},{1... | collective-permute-start | bytes 786440 | tf_op jit(solution)/shard_map/ppermute | solution.py:28
  31.6 0.1 collective-permute-start.14
  31.8 1.7 %collective-permute-start.17 = (bf16[32,4096]{1,0:T(8,128)(2,1)S(1)}, bf16[32,4096]{1,0:T(8,128)(2,1)S(1)}, u32[]{:S(2)}, u32[]{:S(2)}) collective-permute-start(bf16[32,4096]{1,0:T(8,128)(2,1)S(1)} %collective-permute-done.11), channel_id=1, source_target_pairs={{0,4},{1,29},{2,6},{3,31},{4,8},{5,1},{6,10},{7,3},{8,12},{9,5},{1... | collective-permute-start | bytes 786440 | tf_op jit(solution)/shard_map/ppermute | solution.py:28
  33.5 1.2 %collective-permute-start.15 = (bf16[32,4096]{1,0:T(8,128)(2,1)S(1)}, bf16[32,4096]{1,0:T(8,128)(2,1)S(1)}, u32[]{:S(2)}, u32[]{:S(2)}) collective-permute-start(bf16[32,4096]{1,0:T(8,128)(2,1)S(1)} %collective-permute-done.10), channel_id=1, source_target_pairs={{0,2},{1,3},{2,0},{3,1},{4,6},{5,7},{6,4},{7,5},{8,10},{9,11},{10,... | collective-permute-start | bytes 786440 | tf_op jit(solution)/shard_map/ppermute | solution.py:28
  34.8 1.0 collective-permute-done.9
  35.8 2.4 %collective-permute-start.16 = (bf16[128,4096]{1,0:T(8,128)(2,1)S(1)}, bf16[128,4096]{1,0:T(8,128)(2,1)S(1)}, u32[]{:S(2)}, u32[]{:S(2)}) collective-permute-start(bf16[128,4096]{1,0:T(8,128)(2,1)S(1)} %constant_dynamic-update-slice_fusion.4), channel_id=1, source_target_pairs={{0,1},{1,0},{2,3},{3,2},{4,5},{5,4},{6,7},{7,6},{8,9},{9,8},{10,11... | collective-permute-start | bytes 3145736 | tf_op jit(solution)/shard_map/ppermute | solution.py:28
  38.2 0.4 collective-permute-start.18
  38.9 0.1 constant_dynamic-update-slice_fusion.8
  39.0 3.5 %multiply_convert_fusion = f16[384,1024]{1,0:T(8,128)(2,1)S(1)} fusion(bf16[384,4096]{1,0:T(8,128)(2,1)S(1)} %constant_dynamic-update-slice_fusion.8, bf16[4096,1024]{1,0:T(8,128)(2,1)S(1)} %copy-done.3, f32[]{:T(128)S(1)} %bitcast.50), kind=kOutput, calls=%fused_computation.1 | convolution fusion | flops 3222011904 | bytes 12320772 | tf_op jit(solution)/shard_map/dot_general | solution.py:133
  42.5 0.3 pad.4
  42.9 0.4 collective-permute-start.19
  43.3 0.1 constant_dynamic-update-slice_fusion.21
  43.4 2.4 %fusion.2 = f16[1024,1024]{1,0:T(8,128)(2,1)S(1)} fusion(f16[1024,1024]{1,0:T(8,128)(2,1)S(1)} %pad.4, bf16[256,4096]{1,0:T(8,128)(2,1)S(1)} %constant_dynamic-update-slice_fusion.21, bf16[4096,1024]{1,0:T(8,128)(2,1)S(1)} %copy-done.3, f32[]{:T(128)S(1)} %bitcast.51), kind=kOutput, calls=%fused_computation.8 | convolution fusion | flops 2148007936 | bytes 11010560 | tf_op jit(solution)/shard_map/dot_general | solution.py:133
  45.9 0.3 collective-permute-start.20
  46.3 0.1 constant_dynamic-update-slice_fusion.28
  46.4 2.4 %fusion.4 = f16[1024,1024]{1,0:T(8,128)(2,1)S(1)} fusion(f16[1024,1024]{1,0:T(8,128)(2,1)S(1)} %fusion.2, bf16[256,4096]{1,0:T(8,128)(2,1)S(1)} %constant_dynamic-update-slice_fusion.28, bf16[4096,1024]{1,0:T(8,128)(2,1)S(1)} %copy-done.3, f32[]{:T(128)S(1)} %bitcast.52), kind=kOutput, calls=%fused_computation.10 | convolution fusion | flops 2148007936 | bytes 11010560 | tf_op jit(solution)/shard_map/dot_general | solution.py:133
  48.9 0.1 pad_maximum_fusion
  49.0 1.4 %fusion.6 = f16[1024,1024]{1,0:T(8,128)(2,1)S(1)} fusion(f16[1024,1024]{1,0:T(8,128)(2,1)S(1)} %fusion.4, bf16[128,4096]{1,0:T(8,128)(2,1)S(1)} %pad_maximum_fusion, bf16[4096,1024]{1,0:T(8,128)(2,1)S(1)} %copy-done.3, f32[]{:T(128)S(1)} %bitcast.53), kind=kOutput, calls=%fused_computation.13 | convolution fusion | flops 1074003968 | bytes 9699840 | tf_op jit(solution)/shard_map/dot_general | solution.py:133
  50.3 1.3 %copy-done.4 = f16[1024,1024]{1,0:T(8,128)(2,1)} copy-done((f16[1024,1024]{1,0:T(8,128)(2,1)}, f16[1024,1024]{1,0:T(8,128)(2,1)S(1)}, u32[]{:S(2)}) %copy-start.4) | copy-done | bytes 2097176
  51.7 6.6 %all-to-all-start = ((f16[8,128,1024]{2,1,0:T(8,128)(2,1)}), f16[8,128,1024]{2,1,0:T(8,128)(2,1)S(1)}, u32[]{:S(2)}, u32[]{:S(2)}) async-start(f16[8,128,1024]{2,1,0:T(8,128)(2,1)} %bitcast.54), calls=%async_computation | async-start | bytes 4194304 | tf_op jit(solution)/shard_map/all_to_all | solution.py:138
  58.2 0.9 broadcast_subtract_fusion
  59.2 0.3 reshape.60
  59.5 0.3 dot_general.39
  59.8 0.4 reshape.61
  60.2 0.5 convolution_bitcast_fusion.3
  60.7 0.5 convolution_bitcast_fusion.2
  61.2 0.6 convolution_bitcast_fusion.1
  61.8 0.6 fusion
  62.3 0.1 copy.35
  62.4 1.2 %reshape.62 = f32[4,32768]{1,0:T(4,128)} reshape(f32[4,8,64,64]{3,2,1,0:T(8,128)S(1)} %copy.35) | data formatting | bytes 1048576 | tf_op jit(solution)/shard_map/reshape | solution.py:174
  63.7 22.8 %all-to-all-done = f16[8,128,1024]{2,1,0:T(8,128)(2,1)S(1)} async-done(((f16[8,128,1024]{2,1,0:T(8,128)(2,1)}), f16[8,128,1024]{2,1,0:T(8,128)(2,1)S(1)}, u32[]{:S(2)}, u32[]{:S(2)}) %all-to-all-start) | async-done | bytes 2097184 | tf_op jit(solution)/shard_map/all_to_all | solution.py:138
  86.4 0.5 convert_reduce_fusion
  86.9 0.0 copy-start.6
  87.1 0.1 convert_element_type.52
  87.2 19.0 %all_to_all.10 = f16[32,4,1024]{2,1,0:T(4,128)(2,1)S(1)} all-to-all(f16[32,4,1024]{2,1,0:T(4,128)(2,1)S(1)} %convert_element_type.52), channel_id=1, replica_groups=mesh['grp'=8,'mem'=32] {'mem'}, dimensions={0} | all-to-all | bytes 524288 | tf_op jit(solution)/shard_map/all_to_all | solution.py:177
  106.2 0.1 convert_multiply_fusion
  106.3 1.0 add_divide_fusion
  (66 shorter events, 0.8 us)
Async XLA Ops:
  0.0 16.1 %collective-permute-start.1 = (bf16[32,4096]{1,0:T(8,128)(2,1)}, bf16[32,4096]{1,0:T(8,128)(2,1)S(1)}, u32[]{:S(2)}, u32[]{:S(2)}) collective-permute-start(bf16[32,4096]{1,0:T(8,128)(2,1)} %param.10), channel_id=1, source_target_pairs={{0,4},{1,29},{2,6},{3,31},{4,8},{5,1},{6,10},{7,3},{8,12},{9,5},{1... | collective-permute-start | bytes 786440 | tf_op jit(solution)/shard_map/ppermute | solution.py:28
  6.4 9.8 %collective-permute-start.2 = (bf16[32,4096]{1,0:T(8,128)(2,1)}, bf16[32,4096]{1,0:T(8,128)(2,1)S(1)}, u32[]{:S(2)}, u32[]{:S(2)}) collective-permute-start(bf16[32,4096]{1,0:T(8,128)(2,1)} %param.10), channel_id=1, source_target_pairs={{0,1},{1,0},{2,3},{3,2},{4,5},{5,4},{6,7},{7,6},{8,9},{9,8},{10,11... | collective-permute-start | bytes 786440 | tf_op jit(solution)/shard_map/ppermute | solution.py:28
  6.4 9.8 %collective-permute-start = (bf16[32,4096]{1,0:T(8,128)(2,1)}, bf16[32,4096]{1,0:T(8,128)(2,1)S(1)}, u32[]{:S(2)}, u32[]{:S(2)}) collective-permute-start(bf16[32,4096]{1,0:T(8,128)(2,1)} %param.10), channel_id=1, source_target_pairs={{0,29},{1,4},{2,31},{3,6},{4,1},{5,8},{6,3},{7,10},{8,5},{9,12},{1... | collective-permute-start | bytes 786440 | tf_op jit(solution)/shard_map/ppermute | solution.py:28
  6.4 12.2 %collective-permute-start.5 = (bf16[32,4096]{1,0:T(8,128)(2,1)}, bf16[32,4096]{1,0:T(8,128)(2,1)S(1)}, u32[]{:S(2)}, u32[]{:S(2)}) collective-permute-start(bf16[32,4096]{1,0:T(8,128)(2,1)} %param.10), channel_id=1, source_target_pairs={{0,6},{1,31},{2,4},{3,29},{4,10},{5,3},{6,8},{7,1},{8,14},{9,7},{1... | collective-permute-start | bytes 786440 | tf_op jit(solution)/shard_map/ppermute | solution.py:28
  10.4 15.1 %collective-permute-start.8 = (bf16[32,4096]{1,0:T(8,128)(2,1)}, bf16[32,4096]{1,0:T(8,128)(2,1)S(1)}, u32[]{:S(2)}, u32[]{:S(2)}) collective-permute-start(bf16[32,4096]{1,0:T(8,128)(2,1)} %param.10), channel_id=1, source_target_pairs={{0,2},{1,3},{2,0},{3,1},{4,6},{5,7},{6,4},{7,5},{8,10},{9,11},{10,... | collective-permute-start | bytes 786440 | tf_op jit(solution)/shard_map/ppermute | solution.py:28
  13.6 0.7 copy-start
  14.2 0.7 copy-start.1
  14.9 0.7 copy-start.2
  16.1 5.6 %collective-permute-start.4 = (bf16[32,4096]{1,0:T(8,128)(2,1)S(1)}, bf16[32,4096]{1,0:T(8,128)(2,1)S(1)}, u32[]{:S(2)}, u32[]{:S(2)}) collective-permute-start(bf16[32,4096]{1,0:T(8,128)(2,1)S(1)} %collective-permute-done.1), channel_id=1, source_target_pairs={{0,4},{1,29},{2,6},{3,31},{4,8},{5,1},{6,10},{7,3},{8,12},{9,5},{1... | collective-permute-start | bytes 786440 | tf_op jit(solution)/shard_map/ppermute | solution.py:28
  16.3 8.3 %collective-permute-start.3 = (bf16[32,4096]{1,0:T(8,128)(2,1)S(1)}, bf16[32,4096]{1,0:T(8,128)(2,1)S(1)}, u32[]{:S(2)}, u32[]{:S(2)}) collective-permute-start(bf16[32,4096]{1,0:T(8,128)(2,1)S(1)} %collective-permute-done), channel_id=1, source_target_pairs={{0,4},{1,29},{2,6},{3,31},{4,8},{5,1},{6,10},{7,3},{8,12},{9,5},{1... | collective-permute-start | bytes 786440 | tf_op jit(solution)/shard_map/ppermute | solution.py:28
  17.3 14.2 %collective-permute-start.13 = (bf16[32,4096]{1,0:T(8,128)(2,1)S(1)}, bf16[32,4096]{1,0:T(8,128)(2,1)S(1)}, u32[]{:S(2)}, u32[]{:S(2)}) collective-permute-start(bf16[32,4096]{1,0:T(8,128)(2,1)S(1)} %collective-permute-done), channel_id=1, source_target_pairs={{0,2},{1,3},{2,0},{3,1},{4,6},{5,7},{6,4},{7,5},{8,10},{9,11},{10,... | collective-permute-start | bytes 786440 | tf_op jit(solution)/shard_map/ppermute | solution.py:28
  18.6 8.8 %collective-permute-start.7 = (bf16[32,4096]{1,0:T(8,128)(2,1)S(1)}, bf16[32,4096]{1,0:T(8,128)(2,1)S(1)}, u32[]{:S(2)}, u32[]{:S(2)}) collective-permute-start(bf16[32,4096]{1,0:T(8,128)(2,1)S(1)} %collective-permute-done.5), channel_id=1, source_target_pairs={{0,4},{1,29},{2,6},{3,31},{4,8},{5,1},{6,10},{7,3},{8,12},{9,5},{1... | collective-permute-start | bytes 786440 | tf_op jit(solution)/shard_map/ppermute | solution.py:28
  21.2 17.5 %copy-start.9 = (bf16[32,4096]{1,0:T(8,128)(2,1)S(1)}, bf16[32,4096]{1,0:T(8,128)(2,1)}, u32[]{:S(2)}) copy-start(bf16[32,4096]{1,0:T(8,128)(2,1)} %param.10) | copy-start | bytes 786436
  21.7 9.8 %collective-permute-start.11 = (bf16[32,4096]{1,0:T(8,128)(2,1)S(1)}, bf16[32,4096]{1,0:T(8,128)(2,1)S(1)}, u32[]{:S(2)}, u32[]{:S(2)}) collective-permute-start(bf16[32,4096]{1,0:T(8,128)(2,1)S(1)} %collective-permute-done.4), channel_id=1, source_target_pairs={{0,4},{1,29},{2,6},{3,31},{4,8},{5,1},{6,10},{7,3},{8,12},{9,5},{1... | collective-permute-start | bytes 786440 | tf_op jit(solution)/shard_map/ppermute | solution.py:28
  24.6 9.0 %collective-permute-start.10 = (bf16[32,4096]{1,0:T(8,128)(2,1)S(1)}, bf16[32,4096]{1,0:T(8,128)(2,1)S(1)}, u32[]{:S(2)}, u32[]{:S(2)}) collective-permute-start(bf16[32,4096]{1,0:T(8,128)(2,1)S(1)} %collective-permute-done.3), channel_id=1, source_target_pairs={{0,4},{1,29},{2,6},{3,31},{4,8},{5,1},{6,10},{7,3},{8,12},{9,5},{1... | collective-permute-start | bytes 786440 | tf_op jit(solution)/shard_map/ppermute | solution.py:28
  25.5 10.3 %collective-permute-start.6 = (bf16[32,4096]{1,0:T(8,128)(2,1)S(1)}, bf16[32,4096]{1,0:T(8,128)(2,1)S(1)}, u32[]{:S(2)}, u32[]{:S(2)}) collective-permute-start(bf16[32,4096]{1,0:T(8,128)(2,1)S(1)} %collective-permute-done.3), channel_id=1, source_target_pairs={{0,2},{1,3},{2,0},{3,1},{4,6},{5,7},{6,4},{7,5},{8,10},{9,11},{10,... | collective-permute-start | bytes 786440 | tf_op jit(solution)/shard_map/ppermute | solution.py:28
  27.4 2.6 %collective-permute-start.12 = (bf16[32,4096]{1,0:T(8,128)(2,1)S(1)}, bf16[32,4096]{1,0:T(8,128)(2,1)S(1)}, u32[]{:S(2)}, u32[]{:S(2)}) collective-permute-start(bf16[32,4096]{1,0:T(8,128)(2,1)S(1)} %collective-permute-done.8), channel_id=1, source_target_pairs={{0,1},{1,0},{2,3},{3,2},{4,5},{5,4},{6,7},{7,6},{8,9},{9,8},{10,11... | collective-permute-start | bytes 786440 | tf_op jit(solution)/shard_map/ppermute | solution.py:28
  29.9 5.8 %collective-permute-start.9 = (bf16[32,4096]{1,0:T(8,128)(2,1)S(1)}, bf16[32,4096]{1,0:T(8,128)(2,1)S(1)}, u32[]{:S(2)}, u32[]{:S(2)}) collective-permute-start(bf16[32,4096]{1,0:T(8,128)(2,1)S(1)} %collective-permute-done.7), channel_id=1, source_target_pairs={{0,4},{1,29},{2,6},{3,31},{4,8},{5,1},{6,10},{7,3},{8,12},{9,5},{1... | collective-permute-start | bytes 786440 | tf_op jit(solution)/shard_map/ppermute | solution.py:28
  31.6 4.1 %collective-permute-start.14 = (bf16[128,4096]{1,0:T(8,128)(2,1)S(1)}, bf16[128,4096]{1,0:T(8,128)(2,1)S(1)}, u32[]{:S(2)}, u32[]{:S(2)}) collective-permute-start(bf16[128,4096]{1,0:T(8,128)(2,1)S(1)} %constant_dynamic-update-slice_fusion), channel_id=1, source_target_pairs={{0,1},{1,0},{2,3},{3,2},{4,5},{5,4},{6,7},{7,6},{8,9},{9,8},{10,11... | collective-permute-start | bytes 3145736 | tf_op jit(solution)/shard_map/ppermute | solution.py:28
  31.8 14.1 %collective-permute-start.17 = (bf16[32,4096]{1,0:T(8,128)(2,1)S(1)}, bf16[32,4096]{1,0:T(8,128)(2,1)S(1)}, u32[]{:S(2)}, u32[]{:S(2)}) collective-permute-start(bf16[32,4096]{1,0:T(8,128)(2,1)S(1)} %collective-permute-done.11), channel_id=1, source_target_pairs={{0,4},{1,29},{2,6},{3,31},{4,8},{5,1},{6,10},{7,3},{8,12},{9,5},{1... | collective-permute-start | bytes 786440 | tf_op jit(solution)/shard_map/ppermute | solution.py:28
  33.5 9.3 %collective-permute-start.15 = (bf16[32,4096]{1,0:T(8,128)(2,1)S(1)}, bf16[32,4096]{1,0:T(8,128)(2,1)S(1)}, u32[]{:S(2)}, u32[]{:S(2)}) collective-permute-start(bf16[32,4096]{1,0:T(8,128)(2,1)S(1)} %collective-permute-done.10), channel_id=1, source_target_pairs={{0,2},{1,3},{2,0},{3,1},{4,6},{5,7},{6,4},{7,5},{8,10},{9,11},{10,... | collective-permute-start | bytes 786440 | tf_op jit(solution)/shard_map/ppermute | solution.py:28
  34.7 4.2 %copy-start.3 = (bf16[4096,1024]{1,0:T(8,128)(2,1)S(1)}, bf16[4096,1024]{1,0:T(8,128)(2,1)}, u32[]{:S(2)}) copy-start(bf16[4096,1024]{1,0:T(8,128)(2,1)} %param.11) | copy-start | bytes 25165828
  35.8 7.5 %collective-permute-start.16 = (bf16[128,4096]{1,0:T(8,128)(2,1)S(1)}, bf16[128,4096]{1,0:T(8,128)(2,1)S(1)}, u32[]{:S(2)}, u32[]{:S(2)}) collective-permute-start(bf16[128,4096]{1,0:T(8,128)(2,1)S(1)} %constant_dynamic-update-slice_fusion.4), channel_id=1, source_target_pairs={{0,1},{1,0},{2,3},{3,2},{4,5},{5,4},{6,7},{7,6},{8,9},{9,8},{10,11... | collective-permute-start | bytes 3145736 | tf_op jit(solution)/shard_map/ppermute | solution.py:28
  38.2 7.7 %collective-permute-start.18 = (bf16[32,4096]{1,0:T(8,128)(2,1)S(1)}, bf16[32,4096]{1,0:T(8,128)(2,1)S(1)}, u32[]{:S(2)}, u32[]{:S(2)}) collective-permute-start(bf16[32,4096]{1,0:T(8,128)(2,1)S(1)} %collective-permute-done.9), channel_id=1, source_target_pairs={{0,4},{1,29},{2,6},{3,31},{4,8},{5,1},{6,10},{7,3},{8,12},{9,5},{1... | collective-permute-start | bytes 786440 | tf_op jit(solution)/shard_map/ppermute | solution.py:28
  42.9 3.5 %collective-permute-start.19 = (bf16[128,4096]{1,0:T(8,128)(2,1)S(1)}, bf16[128,4096]{1,0:T(8,128)(2,1)S(1)}, u32[]{:S(2)}, u32[]{:S(2)}) collective-permute-start(bf16[128,4096]{1,0:T(8,128)(2,1)S(1)} %constant_dynamic-update-slice_fusion.17), channel_id=1, source_target_pairs={{0,1},{1,0},{2,3},{3,2},{4,5},{5,4},{6,7},{7,6},{8,9},{9,8},{10,11... | collective-permute-start | bytes 3145736 | tf_op jit(solution)/shard_map/ppermute | solution.py:28
  45.9 2.9 %collective-permute-start.20 = (bf16[64,4096]{1,0:T(8,128)(2,1)S(1)}, bf16[64,4096]{1,0:T(8,128)(2,1)S(1)}, u32[]{:S(2)}, u32[]{:S(2)}) collective-permute-start(bf16[64,4096]{1,0:T(8,128)(2,1)S(1)} %constant_dynamic-update-slice_fusion.26), channel_id=1, source_target_pairs={{0,1},{1,0},{2,3},{3,2},{4,5},{5,4},{6,7},{7,6},{8,9},{9,8},{10,11... | collective-permute-start | bytes 1572872 | tf_op jit(solution)/shard_map/ppermute | solution.py:28
  50.3 1.3 %copy-start.4 = (f16[1024,1024]{1,0:T(8,128)(2,1)}, f16[1024,1024]{1,0:T(8,128)(2,1)S(1)}, u32[]{:S(2)}) copy-start(f16[1024,1024]{1,0:T(8,128)(2,1)S(1)} %fusion.6) | copy-start | bytes 6291460
  51.7 7.5 %copy-start.7 = (bf16[19,64,64]{2,1,0:T(8,128)(2,1)S(1)}, bf16[19,64,64]{2,1,0:T(8,128)(2,1)}, u32[]{:S(2)}) copy-start(bf16[19,64,64]{2,1,0:T(8,128)(2,1)} %param.16) | copy-start | bytes 466948
  51.7 8.1 %copy-start.8 = (bf16[4,32768]{1,0:T(4,128)(2,1)S(1)}, bf16[4,32768]{1,0:T(4,128)(2,1)}, u32[]{:S(2)}) copy-start(bf16[4,32768]{1,0:T(4,128)(2,1)} %param.15) | copy-start | bytes 786436
  51.7 34.8 %all-to-all-start = ((f16[8,128,1024]{2,1,0:T(8,128)(2,1)}), f16[8,128,1024]{2,1,0:T(8,128)(2,1)S(1)}, u32[]{:S(2)}, u32[]{:S(2)}) async-start(f16[8,128,1024]{2,1,0:T(8,128)(2,1)} %bitcast.54), calls=%async_computation | async-start | bytes 4194304 | tf_op jit(solution)/shard_map/all_to_all | solution.py:138
  86.9 19.4 %copy-start.5 = (f32[4,32768]{1,0:T(4,128)S(1)}, f32[4,32768]{1,0:T(4,128)}, u32[]{:S(2)}) copy-start(f32[4,32768]{1,0:T(4,128)} %reshape.62) | copy-start | bytes 1572868
  86.9 19.4 %copy-start.6 = (f32[4,32768]{1,0:T(4,128)S(1)}, f32[4,32768]{1,0:T(4,128)}, u32[]{:S(2)}) copy-start(f32[4,32768]{1,0:T(4,128)} %broadcast_subtract_fusion) | copy-start | bytes 1572868
